TPU v7x, 32 devices: a whole 2x2x4 slice. The times are simulated.
32 devices in a mesh: dp: 8 (over y, x, core), tensor: 4 (over z).
Axes of the slice: x: 2, y: 2, z: 4, core: 2. Of those that a mesh axis runs over, the one named last changes fastest.
Arguments:
- hidden_in: bfloat16 [8192, 1024], P(('dp', 'tensor')), may hold values from -6 to 6
- out_grad: bfloat16 [8192, 1024], P(('dp', 'tensor')), may hold values from -6 to 6
- seg_ids: int32 [8192], replicated, may hold values from 0 to 8, as said below
- norm_gain: float32 [1024], replicated, may hold values from 0.1 to 1.9
- gate_weight: bfloat16 [1024, 2048], P('dp', 'tensor'), may hold values from -0.1875 to 0.1875
- value_weight: bfloat16 [1024, 2048], P('dp', 'tensor'), may hold values from -0.1875 to 0.1875
- write_weight: bfloat16 [1024, 128], P('dp', 'tensor'), may hold values from -0.1875 to 0.1875
- read_weight: bfloat16 [1024, 128], P('dp', 'tensor'), may hold values from -0.1875 to 0.1875
- step_weight: bfloat16 [1024, 32], P('dp', 'tensor'), may hold values from -0.1875 to 0.1875
- step_bias: float32 [32], P('tensor'), may hold values from -3 to -1
- decay_log: float32 [32], P('tensor')
- skip_gain: float32 [32], P('tensor'), may hold values from 0.5 to 1.5
- conv_value: float32 [4, 2048], P(None, 'tensor'), may hold values from -3 to 3
- conv_write_read: float32 [2, 4, 128], P(None, None, 'tensor'), may hold values from -3 to 3
- conv_value_bias: float32 [2048], P('tensor'), may hold values from -3 to 3
- conv_write_read_bias: float32 [2, 128], P(None, 'tensor'), may hold values from -3 to 3
- gate_gain: float32 [2048], P('tensor'), may hold values from 0.1 to 1.9
- out_weight: bfloat16 [1024, 2048], P('dp', 'tensor'), may hold values from -0.125 to 0.125
Outputs:
- layer_out: float32 [8192, 1024], P(('dp', 'tensor'))
- input_grad: float32 [8192, 1024], P(('dp', 'tensor'))
- grad_norm_gain: float32 [1024], P('tensor')
- grad_gate_weight: float32 [1024, 2048], P('dp', 'tensor')
- grad_value_weight: float32 [1024, 2048], P('dp', 'tensor')
- grad_write_weight: float32 [1024, 128], P('dp', 'tensor')
- grad_read_weight: float32 [1024, 128], P('dp', 'tensor')
- grad_step_weight: float32 [1024, 32], P('dp', 'tensor')
- grad_step_bias: float32 [32], P('tensor')
- grad_decay_log: float32 [32], P('tensor')
- grad_skip_gain: float32 [32], P('tensor')
- grad_conv_value: float32 [4, 2048], P(None, 'tensor')
- grad_conv_write_read: float32 [2, 4, 128], P(None, None, 'tensor')
- grad_conv_value_bias: float32 [2048], P('tensor')
- grad_conv_write_read_bias: float32 [2, 128], P(None, 'tensor')
- grad_gate_gain: float32 [2048], P('tensor')
- grad_out_weight: float32 [1024, 2048], P('dp', 'tensor')
Inputs may be any that keep to these rules, and one draw needn't show every extreme that they name: `seg_ids`: never falls along the tokens and rises by one where a sequence starts; each block of 1024 tokens holds exactly one start of a sequence away from its first token, so a sequence continues into every block from the one before.
All inputs are finite; a program needn't handle non-finite values.
Results may differ from a plain program's by a relative error of at most 0.0021.
The roundings to bfloat16 on the way count: a program that leaves them out, or rounds other values in their place, can miss the bound.
Values may be sent and summed in bfloat16 or wider, within the bound.
A program may use at most 192 MiB of HBM per device.

v0:
```python
from functools import partial

import jax
import jax.numpy as jnp
from jax import lax
from jax.sharding import PartitionSpec as P

SPAN = 256


epsilon = 1e-05
highest = lax.Precision.HIGHEST


def from_behind(value, axis, steps):
    count = lax.axis_size(axis)
    leading, last = (max(0, -steps), min(count, count - steps))
    return lax.ppermute(value, axis, [(source, source + steps) for source in range(leading, last)])


def entering(part, axis, combine, identity, reverse):
    count = lax.axis_size(axis)
    place = lax.axis_index(axis)
    ahead = count - 1 - place if reverse else place
    gathered = jax.tree.map(lambda a: lax.all_gather(a, axis), part)
    state = jax.tree.map(lambda a, e: jnp.zeros_like(a) + jnp.asarray(e, a.dtype), part, identity)

    def one(lap, state):
        source = count - 1 - lap if reverse else lap
        return combine(
            state, jax.tree.map(lambda a: lax.dynamic_index_in_dim(a, source, 0, False), gathered)
        )

    return lax.fori_loop(0, ahead, one, state)


def span_terms(state, before, values, writes, reads, steps, logs, segment):
    length = segment.shape[0]
    order = jnp.arange(length)
    running = jnp.cumsum(logs, axis=0)
    same = (segment[:, None] == segment[None, :]) & (order[:, None] >= order[None, :])
    gap = running[:, None, :] - running[None, :, :]
    decay = jnp.exp(jnp.where(same[:, :, None], gap, -1e30))
    scores = jnp.dot(reads, writes.T, precision=highest)
    mixing = decay * scores[:, :, None] * steps[None, :, :]
    inner_out = jnp.einsum("tsh,shp->thp", mixing, values, precision=highest)
    carried = segment == before
    entry = jnp.where(carried[:, None], jnp.exp(running), 0.0)
    outer_out = entry[:, :, None] * jnp.einsum("tn,hpn->thp", reads, state, precision=highest)
    ending = segment == segment[-1]
    to_end = jnp.where(ending[:, None], jnp.exp(running[-1][None, :] - running), 0.0) * steps
    written = jnp.einsum("sh,shp,sn->hpn", to_end, values, writes, precision=highest)
    return (entry[-1][:, None, None] * state + written, inner_out + outer_out)


def group_core(values, writes, reads, steps, decay_log, skip_gain, segment, continues, span_size):
    group_rows, heads_here, head_size = values.shape
    state_size = writes.shape[1]
    per_turn = min(group_rows // span_size, max(1, 512 // span_size))
    turns = group_rows // (span_size * per_turn)
    logs = -jnp.exp(decay_log)[None, :] * steps

    def turn_step(carry, block):
        state, before = carry
        outputs = []
        for inner_index in range(per_turn):
            pieces = tuple((item[inner_index] for item in block))
            state, piece_out = span_terms(state, before, *pieces)
            before = pieces[-1][-1]
            outputs.append(piece_out)
        return ((state, before), jnp.stack(outputs))

    blocks = tuple(
        (
            item.reshape((turns, per_turn, span_size) + item.shape[1:])
            for item in (values, writes, reads, steps, logs, segment)
        )
    )
    start = (jnp.zeros((heads_here, head_size, state_size), jnp.float32), segment[0])
    (state_end, _), outputs = lax.scan(turn_step, start, blocks)
    local_out = outputs.reshape(values.shape) + skip_gain[None, :, None] * values
    entry = jnp.where(continues[:, None], jnp.exp(jnp.cumsum(logs, axis=0)), 0.0)
    return (local_out, state_end, entry)


def attach(reads, entry, state_local, state_in):
    extra = entry[:, :, None] * jnp.einsum("tn,hpn->thp", reads, state_in, precision=highest)
    return (extra, entry[-1][:, None, None] * state_in + state_local)


def chain(earlier, later):
    return (earlier[0] * later[0], later[0][:, None, None] * earlier[1] + later[1])


def conv_apply(conv_in, rim, kernel, offset, valid):
    padded = jnp.concatenate([rim, conv_in], axis=0)
    group_rows = conv_in.shape[0]
    width = kernel.shape[0]
    total = offset[None, :]
    for tap_index in range(width):
        begin = width - 1 - tap_index
        total = total + kernel[tap_index][None, :] * jnp.where(
            valid[tap_index][:, None], padded[begin : begin + group_rows], 0.0
        )
    return jax.nn.silu(total)


def contract_last(left, right):
    return lax.dot_general(
        left, right, (((1,), (1,)), ((), ())), preferred_element_type=jnp.float32
    )


def contract_first(left, right):
    return lax.dot_general(
        left, right, (((0,), (0,)), ((), ())), preferred_element_type=jnp.float32
    )


def body(
    hidden_in,
    out_grad,
    seg_ids,
    norm_gain,
    gate_weight,
    value_weight,
    write_weight,
    read_weight,
    step_weight,
    step_bias,
    decay_log,
    skip_gain,
    conv_value,
    conv_write_read,
    conv_value_bias,
    conv_write_read_bias,
    gate_gain,
    out_weight,
):
    tensor_count = lax.axis_size("tensor")
    tensor_rank = lax.axis_index("tensor")
    data_rank = lax.axis_index("dp")
    own_rows = hidden_in.shape[0]
    group_rows = own_rows * tensor_count
    kernel_width = conv_value.shape[0]
    heads_here = step_weight.shape[1]
    inner_here = value_weight.shape[1]
    head_size = inner_here // heads_here
    state_here = write_weight.shape[1]
    state_size = state_here * tensor_count
    inner_total = inner_here * tensor_count
    gate_full, value_full, write_full, read_full, step_full, out_full = (
        lax.all_gather(gate_weight, "dp", axis=0, tiled=True),
        lax.all_gather(value_weight, "dp", axis=0, tiled=True),
        lax.all_gather(write_weight, "dp", axis=0, tiled=True),
        lax.all_gather(read_weight, "dp", axis=0, tiled=True),
        lax.all_gather(step_weight, "dp", axis=0, tiled=True),
        lax.all_gather(out_weight, "dp", axis=0, tiled=True),
    )
    hidden_rows, grad_rows = (
        lax.all_gather(hidden_in, "tensor", axis=0, tiled=True),
        lax.all_gather(out_grad, "tensor", axis=0, tiled=True),
    )
    hidden_float = hidden_rows.astype(jnp.float32)
    scale = lax.rsqrt(jnp.mean(hidden_float * hidden_float, axis=1, keepdims=True) + epsilon)
    normed = hidden_float * scale
    features = (normed * norm_gain[None, :]).astype(jnp.bfloat16)
    conv_full = jnp.concatenate([value_full, write_full, read_full], axis=1)
    gate_in = jnp.dot(features, gate_full, preferred_element_type=jnp.float32)
    conv_in = jnp.dot(features, conv_full, preferred_element_type=jnp.float32)
    step_in = jnp.dot(features, step_full, preferred_element_type=jnp.float32)
    rim = from_behind(conv_in[group_rows - (kernel_width - 1) :], "dp", 1)
    kernel = jnp.concatenate([conv_value, conv_write_read[0], conv_write_read[1]], axis=1)
    offset = jnp.concatenate([conv_value_bias, conv_write_read_bias[0], conv_write_read_bias[1]])
    padded_seg = jnp.concatenate([jnp.full((kernel_width - 1,), -1, jnp.int32), seg_ids])
    window = lax.dynamic_slice_in_dim(
        padded_seg, data_rank * group_rows, group_rows + kernel_width - 1
    )
    segment = window[kernel_width - 1 :]
    valid = jnp.stack(
        [
            window[kernel_width - 1 - tap_index : kernel_width - 1 - tap_index + group_rows]
            == segment
            for tap_index in range(kernel_width)
        ]
    )
    continues = segment == window[kernel_width - 2]
    acted, conv_back = jax.vjp(partial(conv_apply, valid=valid), conv_in, rim, kernel, offset)
    values = acted[:, :inner_here]
    writes_low = acted[:, inner_here : inner_here + state_here].astype(jnp.bfloat16)
    reads_low = acted[:, inner_here + state_here :].astype(jnp.bfloat16)
    writes_all, reads_all = (
        lax.all_gather(writes_low, "tensor", axis=1, tiled=True),
        lax.all_gather(reads_low, "tensor", axis=1, tiled=True),
    )
    writes_float = writes_all.astype(jnp.float32)
    reads_float = reads_all.astype(jnp.float32)
    steps = jax.nn.softplus(step_in + step_bias[None, :])
    head_values = values.reshape(group_rows, heads_here, head_size)
    core_inputs = (head_values, writes_float, reads_float, steps, decay_log, skip_gain)
    core = partial(group_core, segment=segment, continues=continues, span_size=SPAN)
    local_out, state_local, entry = core(*core_inputs)
    unit = (
        jnp.ones((heads_here,), jnp.float32),
        jnp.zeros((heads_here, head_size, state_size), jnp.float32),
    )
    _, state_in = entering((entry[-1], state_local), "dp", chain, unit, False)
    (extra, _), attach_back = jax.vjp(attach, reads_float, entry, state_local, state_in)
    mixed = (local_out + extra).reshape(group_rows, inner_here)
    gate_act = jax.nn.silu(gate_in)
    gated = mixed * gate_act
    squares = lax.psum(jnp.sum(gated * gated, axis=1), "tensor")
    rms = lax.rsqrt(squares / inner_total + epsilon)
    branch = (gated * rms[:, None] * gate_gain[None, :]).astype(jnp.bfloat16)
    summed = lax.psum_scatter(
        contract_last(branch, out_full), "tensor", scatter_dimension=0, tiled=True
    )
    layer_out = hidden_in.astype(jnp.float32) + summed
    branch_grad = jnp.dot(grad_rows, out_full, preferred_element_type=jnp.float32)
    out_weight_grad = contract_first(grad_rows, branch)
    gate_gain_grad = jnp.sum(branch_grad * gated * rms[:, None], axis=0)
    scaled = branch_grad * gate_gain[None, :]
    dots = lax.psum(jnp.sum(scaled * gated, axis=1), "tensor")
    gated_grad = rms[:, None] * scaled - gated * (rms * rms * rms * dots / inner_total)[:, None]
    mixed_grad = gated_grad * gate_act
    gate_sigmoid = jax.nn.sigmoid(gate_in)
    gate_grad = gated_grad * mixed * gate_sigmoid * (1.0 + gate_in * (1.0 - gate_sigmoid))
    head_grad = mixed_grad.reshape(group_rows, heads_here, head_size)
    carry_term = jnp.einsum("th,thp,tn->hpn", entry, head_grad, reads_float, precision=highest)
    _, state_out_grad = entering((entry[-1], carry_term), "dp", chain, unit, True)
    reads_extra_grad, entry_grad, state_local_grad, _ = attach_back((head_grad, state_out_grad))
    _, core_back = jax.vjp(core, *core_inputs)
    values_grad, writes_grad, reads_grad, steps_grad, decay_log_grad, skip_grad = core_back(
        (head_grad, state_local_grad, entry_grad)
    )
    reads_grad = reads_grad + reads_extra_grad
    write_part, read_part = (
        lax.psum_scatter(writes_grad, "tensor", scatter_dimension=1, tiled=True),
        lax.psum_scatter(reads_grad, "tensor", scatter_dimension=1, tiled=True),
    )
    acted_grad = jnp.concatenate(
        [values_grad.reshape(group_rows, inner_here), write_part, read_part], axis=1
    )
    conv_in_grad, rim_grad, kernel_grad, offset_grad = conv_back(acted_grad)
    rim_return = from_behind(rim_grad, "dp", -1)
    edge = group_rows - (kernel_width - 1)
    conv_in_grad = jnp.concatenate([conv_in_grad[:edge], conv_in_grad[edge:] + rim_return], axis=0)
    step_pre = steps_grad * jax.nn.sigmoid(step_in + step_bias[None, :])
    step_bias_grad = jnp.sum(step_pre, axis=0)
    gate_low = gate_grad.astype(jnp.bfloat16)
    conv_low = conv_in_grad.astype(jnp.bfloat16)
    step_low = step_pre.astype(jnp.bfloat16)
    features_grad = (
        contract_last(gate_low, gate_full)
        + contract_last(conv_low, conv_full)
        + contract_last(step_low, step_full)
    )
    gain_part = jnp.sum(features_grad * normed, axis=0)
    own_features_grad, norm_gain_grad = (
        lax.psum_scatter(features_grad, "tensor", scatter_dimension=0, tiled=True),
        lax.psum_scatter(gain_part, "tensor", scatter_dimension=0, tiled=True),
    )
    own_normed = lax.dynamic_slice_in_dim(normed, tensor_rank * own_rows, own_rows, 0)
    own_scale = lax.dynamic_slice_in_dim(scale, tensor_rank * own_rows, own_rows, 0)
    normed_grad = own_features_grad * norm_gain[None, :]
    input_grad = out_grad.astype(jnp.float32) + own_scale * (
        normed_grad - own_normed * jnp.mean(normed_grad * own_normed, axis=1, keepdims=True)
    )
    gate_weight_grad = contract_first(features, gate_low)
    conv_weight_grad = contract_first(features, conv_low)
    step_weight_grad = contract_first(features, step_low)
    weight_sums = (
        lax.psum_scatter(gate_weight_grad, "dp", scatter_dimension=0, tiled=True),
        lax.psum_scatter(conv_weight_grad[:, :inner_here], "dp", scatter_dimension=0, tiled=True),
        lax.psum_scatter(
            conv_weight_grad[:, inner_here : inner_here + state_here],
            "dp",
            scatter_dimension=0,
            tiled=True,
        ),
        lax.psum_scatter(
            conv_weight_grad[:, inner_here + state_here :], "dp", scatter_dimension=0, tiled=True
        ),
        lax.psum_scatter(step_weight_grad, "dp", scatter_dimension=0, tiled=True),
        lax.psum_scatter(out_weight_grad, "dp", scatter_dimension=0, tiled=True),
    )
    conv_value_grad = kernel_grad[:, :inner_here]
    conv_pair_grad = jnp.stack(
        [
            kernel_grad[:, inner_here : inner_here + state_here],
            kernel_grad[:, inner_here + state_here :],
        ]
    )
    conv_value_bias_grad = offset_grad[:inner_here]
    conv_pair_bias_grad = jnp.stack(
        [offset_grad[inner_here : inner_here + state_here], offset_grad[inner_here + state_here :]]
    )
    small_sums = lax.psum(
        (
            norm_gain_grad,
            gate_gain_grad,
            step_bias_grad,
            decay_log_grad,
            skip_grad,
            conv_value_grad,
            conv_pair_grad,
            conv_value_bias_grad,
            conv_pair_bias_grad,
        ),
        "dp",
    )
    return (
        layer_out,
        input_grad,
        small_sums[0],
        weight_sums[0],
        weight_sums[1],
        weight_sums[2],
        weight_sums[3],
        weight_sums[4],
        small_sums[2],
        small_sums[3],
        small_sums[4],
        small_sums[5],
        small_sums[6],
        small_sums[7],
        small_sums[8],
        small_sums[1],
        weight_sums[5],
    )


def solution(mesh):
    return jax.shard_map(
        body,
        mesh=mesh,
        in_specs=(
            P(("dp", "tensor"), None),
            P(("dp", "tensor"), None),
            P(),
            P(),
            P("dp", "tensor"),
            P("dp", "tensor"),
            P("dp", "tensor"),
            P("dp", "tensor"),
            P("dp", "tensor"),
            P("tensor"),
            P("tensor"),
            P("tensor"),
            P(None, "tensor"),
            P(None, None, "tensor"),
            P("tensor"),
            P(None, "tensor"),
            P("tensor"),
            P("dp", "tensor"),
        ),
        out_specs=(
            P(("dp", "tensor"), None),
            P(("dp", "tensor"), None),
            P("tensor"),
            P("dp", "tensor"),
            P("dp", "tensor"),
            P("dp", "tensor"),
            P("dp", "tensor"),
            P("dp", "tensor"),
            P("tensor"),
            P("tensor"),
            P("tensor"),
            P(None, "tensor"),
            P(None, None, "tensor"),
            P("tensor"),
            P(None, "tensor"),
            P("tensor"),
            P("dp", "tensor"),
        ),
        check_vma=False,
    )
```

profile of v0, /device:TPU:10, one launch (start us, length us, event | category | flops | bytes accessed | tf_op | source)
XLA Modules:
  0.0 1018.5 jit_solution(2831969245510700369)
XLA Ops:
  8.7 8.9 all_gather.49
  43.6 11.5 %all-gather.11.cloned.1.call-done = bf16[1024,1024]{1,0:T(8,128)(2,1)} async-done(((bf16[256,1024]{1,0:T(8,128)(2,1)}), bf16[1024,1024]{1,0:T(8,128)(2,1)}) %all-gather.11.cloned.1.call-update) | async-done | bytes 2097168 | tf_op jit(solution)/shard_map/all_gather | solution.py:161
  57.4 23.5 %all-gather.13.cloned.1.call-done = bf16[1024,512]{1,0:T(8,128)(2,1)} async-done(((bf16[128,512]{1,0:T(8,128)(2,1)}), bf16[1024,512]{1,0:T(8,128)(2,1)}) %all-gather.13.cloned.1.call-update) | async-done | bytes 1048592 | tf_op jit(solution)/shard_map/all_gather | solution.py:154
  96.2 13.9 %all_gather.52 = bf16[1024,128]{0,1:T(8,128)(2,1)S(1)} all-gather(bf16[1024,32]{0,1:T(8,128)(2,1)S(1)} %get-tuple-element.3261), channel_id=1, replica_groups=mesh['dp'=8,'tensor'=4] {'tensor'}, dimensions={1}, use_global_device_ids=true | all-gather | bytes 327680 | tf_op jit(solution)/shard_map/all_gather | solution.py:194
  118.6 14.8 %all_gather.51 = bf16[1024,128]{0,1:T(8,128)(2,1)} all-gather(bf16[1024,32]{0,1:T(8,128)(2,1)S(1)} %get-tuple-element.3262), channel_id=1, replica_groups=mesh['dp'=8,'tensor'=4] {'tensor'}, dimensions={1}, use_global_device_ids=true | all-gather | bytes 327680 | tf_op jit(solution)/shard_map/all_gather | solution.py:193
  136.5 43.2 %while.172 = (s32[]{:T(128)}, f32[8,64,128]{2,1,0:T(8,128)S(1)}, s32[]{:T(128)}, f32[2,2,256,8,64]{2,1,0,4,3:T(2,128)}, s32[2,2,256]{2,1,0:T(2,128)}, /*index=5*...) while((s32[]{:T(128)}, f32[8,64,128]{2,1,0:T(8,128)S(1)}, ...), condition=%wide.region_6.7_spmd.clone, body=%wide.region_1.6_spmd.clone.sunk | while | flops 1818510336 | bytes 30427740 | solution.py:80
  198.4 11.0 %all-gather.21.cloned.1.call-done = f32[64,64,128]{2,1,0:T(8,128)} async-done(((f32[8,64,128]{2,1,0:T(8,128)}), f32[64,64,128]{2,1,0:T(8,128)}) %all-gather.21.cloned.1.call-update) | async-done | bytes 2097168 | tf_op jit(solution)/shard_map/all_gather | solution.py:25
  221.2 13.4 %all-gather.15.cloned.1.call-done = bf16[1024,512]{1,0:T(8,128)(2,1)} async-done(((bf16[128,512]{1,0:T(8,128)(2,1)}), bf16[1024,512]{1,0:T(8,128)(2,1)}) %all-gather.15.cloned.1.call-update) | async-done | bytes 1048592 | tf_op jit(solution)/shard_map/all_gather | solution.py:153
  249.8 10.0 all-gather.17.cloned.1.call-done
  259.9 45.8 %all-gather.19.cloned.1.call-done = bf16[1024,1024]{1,0:T(8,128)(2,1)} async-done(((bf16[256,1024]{1,0:T(8,128)(2,1)}), bf16[1024,1024]{1,0:T(8,128)(2,1)}) %all-gather.19.cloned.1.call-update) | async-done | bytes 2097168 | tf_op jit(solution)/shard_map/all_gather | solution.py:162
  311.6 10.4 %psum.78 = f32[1024]{0:T(1024)S(1)} all-reduce(f32[1024]{0:T(1024)S(1)} %get-tuple-element.2856), channel_id=1, replica_groups=mesh['dp'=8,'tensor'=4] {'tensor'}, use_global_device_ids=true, to_apply=%region_15.16 | all-reduce | flops 1024 | bytes 8192 | tf_op jit(solution)/shard_map/psum | solution.py:223
  331.9 70.0 %while.173 = (s32[]{:T(128)}, f32[8,64,128]{2,1,0:T(8,128)S(1)}, s32[]{:T(128)}, pred[2,256,256,8]{2,3,1,0:T(8,128)(4,1)}, f32[2,256,256,8]{2,3,1,0:T(8,128)}, /...) while((s32[]{:T(128)}, f32[8,64,128]{2,1,0:T(8,128)S(1)}, ...), condition=%wide.region_23.24_spmd.clone.clone, body=%wide.region_18.23_spmd.clone.clone.sunk | while | flops 1012745280 | bytes 56234484 | solution.py:80
  419.7 141.3 %while.171 = (s32[]{:T(128)}, f32[8,64,128]{2,1,0:T(8,128)S(1)}, f32[2,2,256,8,64]{2,1,0,4,3:T(2,128)}, f32[2,2,256,128]{3,2,1,0:T(8,128)}, f32[2,2,256,128]{3,2...) while((s32[]{:T(128)}, f32[8,64,128]{2,1,0:T(8,128)S(1)}, ...), condition=%wide.region_43.44_spmd, body=%wide.region_24.43_spmd.sunk | while | flops 3637952512 | bytes 171259728 | solution.py:80
  585.7 22.3 %reduce-scatter.13.cloned.1.call-done = f32[1024,32]{0,1:T(8,128)} async-done(((f32[1024,128]{0,1:T(8,128)}), f32[1024,32]{0,1:T(8,128)}) %reduce-scatter.13.cloned.1.call-update) | async-done | bytes 131088 | tf_op jit(solution)/shard_map/reduce_scatter | solution.py:238
  608.0 9.3 multiply_reduce_fusion.6
  642.4 9.9 reduce-window.114
  673.7 11.9 %all-reduce.24 = f32[1024]{0:T(1024)S(1)} all-reduce(f32[1024]{0:T(1024)S(1)} %get-tuple-element.3259), channel_id=8, replica_groups=mesh['dp'=8,'tensor'=4] {'tensor'}, use_global_device_ids=true, to_apply=%region_53.54.clone | all-reduce | flops 1024 | bytes 8192
  685.7 20.8 %all-reduce.25 = (f32[256]{0:T(256)}, f32[8]{0:T(128)}, f32[8]{0:T(128)}, f32[8]{0:T(128)}, f32[4,512]{1,0:T(4,128)}, /*index=5*/f32[2,4,32]{2,1,0:T(4,128)}, f32[512]{0:T(512)}, f32[2,32]{1,0:T(2,128)}, f32[512]{0:T(512)}) all-reduce(f32[256]{0:T(256)S(1)} %dynamic-slice.5, ...), channel_id=1, replica_groups=mesh['dp'=8,'tensor'=4] {'dp'}, use_global_device_ids=true, to_apply=%region_54.55 | all-reduce | flops 3672 | bytes 29376 | tf_op jit(solution)/shard_map/psum | solution.py:298
  708.4 69.3 %reduce-scatter.11.cloned.1.call-done = f32[256,1024]{1,0:T(8,128)} async-done(((f32[1024,1024]{1,0:T(8,128)}), f32[256,1024]{1,0:T(8,128)}) %reduce-scatter.11.cloned.1.call-update) | async-done | bytes 1048592 | tf_op jit(solution)/shard_map/reduce_scatter | solution.py:215
  780.0 77.3 %reduce-scatter.17.cloned.1.call-done = f32[256,1024]{1,0:T(8,128)} async-done(((f32[1024,1024]{1,0:T(8,128)}), f32[256,1024]{1,0:T(8,128)}) %reduce-scatter.17.cloned.1.call-update) | async-done | bytes 1048592 | tf_op jit(solution)/shard_map/reduce_scatter | solution.py:260
  861.7 41.1 %reduce-scatter.19.cloned.1.call-done = f32[128,512]{1,0:T(8,128)} async-done(((f32[1024,512]{1,0:T(8,128)}), f32[128,512]{1,0:T(8,128)}) %reduce-scatter.19.cloned.1.call-update) | async-done | bytes 262160 | tf_op jit(solution)/shard_map/reduce_scatter | solution.py:273
  902.8 35.0 %reduce-scatter.27.cloned.1.call-done = f32[128,8]{0,1:T(8,128)} async-done(((f32[1024,8]{0,1:T(8,128)}), f32[128,8]{0,1:T(8,128)}) %reduce-scatter.27.cloned.1.call-update) | async-done | bytes 4112 | tf_op jit(solution)/shard_map/reduce_scatter | solution.py:284
  937.8 36.8 %reduce-scatter.23.cloned.1.call-done = f32[128,32]{0,1:T(8,128)} async-done(((f32[1024,32]{0,1:T(8,128)}), f32[128,32]{0,1:T(8,128)}) %reduce-scatter.23.cloned.1.call-update) | async-done | bytes 16400 | tf_op jit(solution)/shard_map/reduce_scatter | solution.py:275
  974.6 37.1 %reduce-scatter.25.cloned.1.call-done = f32[128,32]{0,1:T(8,128)} async-done(((f32[1024,32]{0,1:T(8,128)}), f32[128,32]{0,1:T(8,128)}) %reduce-scatter.25.cloned.1.call-update) | async-done | bytes 16400 | tf_op jit(solution)/shard_map/reduce_scatter | solution.py:281
  (849 shorter events, 467.0 us)
Async XLA Ops:
  7.2 47.9 %all-gather.11.cloned.1.call-start = ((), (), s32[]{:S(2)}) async-start(), calls=%async_computation.10 | async-start | bytes 2621440 | tf_op jit(solution)/shard_map/all_gather | solution.py:161
  7.9 72.9 %all-gather.13.cloned.1.call-start = ((), (), s32[]{:S(2)}) async-start(), calls=%async_computation.11 | async-start | bytes 1179648 | tf_op jit(solution)/shard_map/all_gather | solution.py:154
  8.7 200.7 %all-gather.21.cloned.1.call-start = ((), (), s32[]{:S(2)}) async-start(), calls=%async_computation.25 | async-start | bytes 2359296 | tf_op jit(solution)/shard_map/all_gather | solution.py:25
  57.3 177.3 %copy-start.101 = (f32[1024]{0:T(1024)}, f32[1024]{0:T(1024)S(1)}, u32[]{:S(2)}) copy-start(f32[1024]{0:T(1024)S(1)} %add_rsqrt_fusion.1) | copy-start | bytes 12292
  83.9 8.0 collective-permute-start
  180.4 54.2 %all-gather.15.cloned.1.call-start = ((), (), s32[]{:S(2)}) async-start(), calls=%async_computation.12 | async-start | bytes 1179648 | tf_op jit(solution)/shard_map/all_gather | solution.py:153
  181.0 78.8 %all-gather.17.cloned.1.call-start = ((), (), s32[]{:S(2)}) async-start(), calls=%async_computation.13 | async-start | bytes 1179648 | tf_op jit(solution)/shard_map/all_gather | solution.py:158
  181.6 124.0 %all-gather.19.cloned.1.call-start = ((), (), s32[]{:S(2)}) async-start(), calls=%async_computation.15 | async-start | bytes 2621440 | tf_op jit(solution)/shard_map/all_gather | solution.py:162
  182.2 223.7 %all-gather.23.cloned.1.call-start = ((), (), s32[]{:S(2)}) async-start(), calls=%async_computation.26 | async-start | bytes 2359296 | tf_op jit(solution)/shard_map/all_gather | solution.py:25
  186.1 142.1 %copy-start.60 = (f32[1024,8]{0,1:T(8,128)}, f32[1024,8]{0,1:T(8,128)S(1)}, u32[]{:S(2)}) copy-start(f32[1024,8]{0,1:T(8,128)S(1)} %fusion.294) | copy-start | bytes 98308
  331.4 254.3 %reduce-scatter.15.cloned.1.call-start = ((), (), s32[]{:S(2)}) async-start(), calls=%async_computation.17 | async-start | bytes 655360 | tf_op jit(solution)/shard_map/reduce_scatter | solution.py:239
  419.6 142.6 %copy-start.7 = (f32[8,64,128]{2,1,0:T(8,128)S(1)}, f32[8,64,128]{2,1,0:T(8,128)}, u32[]{:S(2)}) copy-start(f32[8,64,128]{2,1,0:T(8,128)} %get-tuple-element.1823) | copy-start | bytes 786436
  419.6 142.6 %copy-start.61 = (f32[1024,8]{0,1:T(8,128)S(1)}, f32[1024,8]{0,1:T(8,128)}, u32[]{:S(2)}) copy-start(f32[1024,8]{0,1:T(8,128)} %copy-done.60) | copy-start | bytes 98308
  566.2 41.7 %reduce-scatter.13.cloned.1.call-start = ((), (), s32[]{:S(2)}) async-start(), calls=%async_computation.16 | async-start | bytes 655360 | tf_op jit(solution)/shard_map/reduce_scatter | solution.py:238
  567.3 101.0 %reduce-scatter.29.cloned.1.call-start = ((), (), s32[]{:S(2)}) async-start(), calls=%async_computation.24 | async-start | bytes 2359296 | tf_op jit(solution)/shard_map/reduce_scatter | solution.py:285
  571.6 134.9 %reduce-scatter.21.cloned.1.call-start = ((), (), s32[]{:S(2)}) async-start(), calls=%async_computation.20 | async-start | bytes 2359296 | tf_op jit(solution)/shard_map/reduce_scatter | solution.py:274
  618.3 6.1 collective-permute-start.1
  629.6 148.1 %reduce-scatter.11.cloned.1.call-start = ((), (), s32[]{:S(2)}) async-start(), calls=%async_computation.14 | async-start | bytes 5242880 | tf_op jit(solution)/shard_map/reduce_scatter | solution.py:215
  635.8 221.5 %reduce-scatter.17.cloned.1.call-start = ((), (), s32[]{:S(2)}) async-start(), calls=%async_computation.18 | async-start | bytes 5242880 | tf_op jit(solution)/shard_map/reduce_scatter | solution.py:260
  662.0 240.8 %reduce-scatter.19.cloned.1.call-start = ((), (), s32[]{:S(2)}) async-start(), calls=%async_computation.19 | async-start | bytes 2359296 | tf_op jit(solution)/shard_map/reduce_scatter | solution.py:273
  666.2 271.6 %reduce-scatter.27.cloned.1.call-start = ((), (), s32[]{:S(2)}) async-start(), calls=%async_computation.23 | async-start | bytes 36864 | tf_op jit(solution)/shard_map/reduce_scatter | solution.py:284
  671.5 303.1 %reduce-scatter.23.cloned.1.call-start = ((), (), s32[]{:S(2)}) async-start(), calls=%async_computation.21 | async-start | bytes 147456 | tf_op jit(solution)/shard_map/reduce_scatter | solution.py:275
  673.6 338.1 %reduce-scatter.25.cloned.1.call-start = ((), (), s32[]{:S(2)}) async-start(), calls=%async_computation.22 | async-start | bytes 147456 | tf_op jit(solution)/shard_map/reduce_scatter | solution.py:281
  708.4 150.8 %copy-start.45 = (bf16[256,1024]{1,0:T(8,128)(2,1)S(1)}, bf16[256,1024]{1,0:T(8,128)(2,1)}, u32[]{:S(2)}) copy-start(bf16[256,1024]{1,0:T(8,128)(2,1)} %param.29) | copy-start | bytes 1572868
  (184 other events, 2074.1 us)
Sparse Core Ops, SparseCore 0:
  9.6 45.4 all-gather.10
  57.0 23.7 all-gather.12
  180.6 28.7 all-gather.20
  211.1 23.4 all-gather.14
  236.3 23.4 all-gather.16
  261.3 44.3 all-gather.18
  331.5 27.1 all-gather.22
  566.4 19.2 reduce-scatter.14
  588.0 19.9 reduce-scatter.12
  611.1 42.5 reduce-scatter.28
  657.4 41.2 reduce-scatter.20
  700.8 76.8 reduce-scatter.10
  780.0 77.2 reduce-scatter.16
  861.1 41.6 reduce-scatter.18
  906.5 31.2 reduce-scatter.26
  941.2 33.3 reduce-scatter.22
  978.3 33.3 reduce-scatter.24
where the time goes:
time: 1030 us; the launch traced here: 1020 us
  waiting for transfers between devices  449 us (44%)
  matrix products  151 us (15%)
  local copies, waits for them, and re-layouts  141 us (14%)
  other arithmetic  126 us (12%)
  blocking collectives  115 us (11%)
  between operations  16.9 us (2%)
  loops' own time  13.2 us (1%)
    reduce_scatter x1, waiting for transfers between devices, body(): lax.psum_scatter(features_grad, 'tensor', scatter_dimension=0, tiled=True)  77.3 us
    reduce_scatter x1, waiting for transfers between devices, body(): lax.psum_scatter(contract_last(branch, out_full), 'tensor', scatter_dimen...  69.3 us
    all_gather x1, waiting for transfers between devices, body(): lax.all_gather(out_grad, 'tensor', axis=0, tiled=True)  45.8 us
    reduce_scatter x1, waiting for transfers between devices, body(): lax.psum_scatter(gate_weight_grad, 'dp', scatter_dimension=0, tiled=True)  41.1 us
    dot_general x12, matrix products, span_terms(): inner_out = jnp.einsum('tsh,shp->thp', mixing, values, precision=highest)  39 us
    reduce_scatter x1, waiting for transfers between devices, body(): lax.psum_scatter(conv_weight_grad[:, inner_here + state_here:], 'dp', sca...  37.1 us
    reduce_scatter x1, waiting for transfers between devices, body(): lax.psum_scatter(conv_weight_grad[:, inner_here:inner_here + state_here],...  36.8 us
    another operation x80, other arithmetic  35.3 us
  transfers between devices with their start and end apart: 19, of which 16 were waited for; matrix products, arithmetic and copies ran while one was open for 17% of the time, Pallas kernels for 0%

commit v1 on v0

v1 whole, which is shorter than its diff:
```python
from functools import partial

import jax
import jax.numpy as jnp
from jax import lax
from jax.experimental import pallas as pl
from jax.experimental.pallas import tpu as pltpu
from jax.sharding import PartitionSpec as P

SPAN = 128


epsilon = 1e-05
highest = lax.Precision.HIGHEST


def from_behind(value, axis, steps):
    count = lax.axis_size(axis)
    leading, last = (max(0, -steps), min(count, count - steps))
    return lax.ppermute(value, axis, [(source, source + steps) for source in range(leading, last)])


def product(left, right, left_dim=1, right_dim=0):
    return lax.dot_general(
        left, right, (((left_dim,), (right_dim,)), ((), ())), preferred_element_type=jnp.float32
    )


def pieces_of(value, count):
    pieces = []
    for _ in range(count - 1):
        piece = value.astype(jnp.bfloat16)
        pieces.append(piece)
        value = value - piece.astype(jnp.float32)
    return pieces + [value.astype(jnp.bfloat16)]


def exact_left(left, right, count, left_dim=1, right_dim=0):
    return sum(product(left, piece, left_dim, right_dim) for piece in pieces_of(right, count))


def exact_right(left, right, count, left_dim=1, right_dim=0):
    return sum(product(piece, right, left_dim, right_dim) for piece in pieces_of(left, count))


def split_product(left, right, left_dim=1, right_dim=0):
    left_high, left_rest = pieces_of(left, 2)
    right_high, right_rest = pieces_of(right, 2)
    return (
        product(left_high, right_high, left_dim, right_dim)
        + product(left_high, right_rest, left_dim, right_dim)
        + product(left_rest, right_high, left_dim, right_dim)
    )


def ones_where(condition):
    return jnp.where(condition, 1.0, 0.0).astype(jnp.bfloat16)


def span_index(length):
    row = lax.broadcasted_iota(jnp.int32, (length, length), 0)
    column = lax.broadcasted_iota(jnp.int32, (length, length), 1)
    return row, column


def head_map(heads, width):
    head = lax.broadcasted_iota(jnp.int32, (heads, width), 0)
    lane = lax.broadcasted_iota(jnp.int32, (heads, width), 1)
    return ones_where(lane // (width // heads) == head)


def decays(row, column, steps, rate, seg, seg_before):
    length = steps.shape[0]
    running = exact_left(ones_where(row >= column), steps * rate, 3)
    entry = jnp.where(seg == seg_before[0:1], jnp.exp(running), 0.0)
    to_end = jnp.where(
        seg == seg[length - 1 : length], jnp.exp(running[length - 1 : length] - running), 0.0
    )
    return running, entry, to_end


def state_kernel(values, writes, steps, rate, seg, seg_before, state):
    length, width = values.shape
    heads = steps.shape[1]

    @pl.when(pl.program_id(0) == 0)
    def _():
        state[...] = jnp.zeros_like(state)

    row, column = span_index(length)
    expand = head_map(heads, width)
    step = steps[...]
    _, entry, to_end = decays(row, column, step, rate[...], seg[...], seg_before[...])
    weighted = exact_right(to_end * step, expand, 3) * values[...]
    kept = exact_right(jnp.broadcast_to(entry[length - 1 :], (8, heads)), expand, 3)[0:1]
    state[...] = kept * state[...] + exact_left(writes[...], weighted, 2, 0, 0)


def forward_kernel(
    values, writes, reads, steps, steps_row, rate, rate_row, seg, seg_row, seg_before, seg_group,
    skip, state_in, mixed, states, entries, state, total,
):
    length, width = values.shape
    heads = steps.shape[1]
    pair = 2 * (width // heads)

    @pl.when(pl.program_id(0) == 0)
    def _():
        state[...] = state_in[...]
        total[...] = jnp.zeros_like(total)

    row, column = span_index(length)
    expand = head_map(heads, width)
    step = steps[...]
    step_row = steps_row[...]
    running, entry, to_end = decays(row, column, step, rate[...], seg[...], seg_before[...])
    running_row = exact_right(step_row * rate_row[...], ones_where(row <= column), 3)
    same = (seg[...] == seg_row[...]) & (row >= column)
    scores = product(reads[...], writes[...], 1, 1)
    before = state[...]
    states[0] = before
    outer = exact_right(entry, expand, 3) * exact_left(reads[...], before, 2)
    lane = lax.broadcasted_iota(jnp.int32, (length, pair), 1)
    for j in range(heads // 2):
        lanes = slice(j * pair, (j + 1) * pair)
        value = values[:, lanes]
        mixing = []
        for h in (2 * j, 2 * j + 1):
            gap = running[:, h : h + 1] - running_row[h : h + 1, :]
            mixing.append(
                jnp.exp(jnp.where(same, gap, -1e30)) * scores * step_row[h : h + 1, :]
            )
        stacked = jnp.concatenate(
            [jnp.where(lane < pair // 2, value, 0.0), jnp.where(lane >= pair // 2, value, 0.0)],
            axis=0,
        )
        mixed[:, lanes] = (
            split_product(jnp.concatenate(mixing, axis=1), stacked)
            + outer[:, lanes]
            + skip[:, lanes] * value
        )
    weighted = exact_right(to_end * step, expand, 3) * values[...]
    kept = exact_right(jnp.broadcast_to(entry[length - 1 :], (8, heads)), expand, 3)[0:1]
    state[...] = kept * before + exact_left(writes[...], weighted, 2, 0, 0)
    whole = total[...] + running
    total[...] = whole[length - 1 :]
    entries[...] = exact_right(
        jnp.where(seg[...] == seg_group[...], jnp.exp(whole), 0.0), expand, 3
    )


def backward_kernel(
    values, grads, writes, reads, steps, steps_row, rate, rate_row, seg, seg_row, seg_before,
    skip, states, adjoint_in, values_grad, writes_grad, reads_grad, steps_grad, decay_grad,
    skip_grad, adjoint,
):
    length, width = values.shape
    heads = steps.shape[1]
    pair = 2 * (width // heads)

    @pl.when(pl.program_id(0) == 0)
    def _():
        adjoint[...] = adjoint_in[...]
        decay_grad[...] = jnp.zeros_like(decay_grad)
        skip_grad[...] = jnp.zeros_like(skip_grad)

    row, column = span_index(length)
    expand = head_map(heads, width)
    step = steps[...]
    running, entry, to_end = decays(row, column, step, rate[...], seg[...], seg_before[...])
    running_row = exact_right(steps_row[...] * rate_row[...], ones_where(row <= column), 3)
    same = (seg[...] == seg_row[...]) & (row <= column)
    write = writes[...]
    read = reads[...]
    scores = product(write, read, 1, 1)
    later = adjoint[...]
    before = states[0]
    grad = grads[...]
    value = values[...]
    weight = to_end * step
    weights = exact_right(weight, expand, 3)
    entered = exact_right(entry, expand, 3) * grad
    arriving = exact_left(write, later, 2)
    scores_grad = jnp.zeros((length, length), jnp.float32)
    lane = lax.broadcasted_iota(jnp.int32, (length, pair), 1)
    head_lane = lax.broadcasted_iota(jnp.int32, (length, heads), 1)
    source_sums = jnp.zeros((length, heads), jnp.float32)
    target_sums = []
    for j in range(heads // 2):
        lanes = slice(j * pair, (j + 1) * pair)
        grad_pair = grads[:, lanes]
        value_pair = values[:, lanes]
        mixing = []
        halves = []
        for h in (2 * j, 2 * j + 1):
            mine = (lane < pair // 2) if h % 2 == 0 else (lane >= pair // 2)
            decay = jnp.exp(jnp.where(same, running_row[h : h + 1, :] - running[:, h : h + 1], -1e30))
            stepped = decay * step[:, h : h + 1]
            mixing.append(stepped * scores)
            mixing_grad = split_product(jnp.where(mine, value_pair, 0.0), grad_pair, 1, 1)
            stepped_grad = mixing_grad * stepped
            scores_grad = scores_grad + stepped_grad
            source = jnp.sum(mixing_grad * (decay * scores), axis=1, keepdims=True)
            source_sums = jnp.where(head_lane == h, source, source_sums)
            target_sums.append(jnp.sum(stepped_grad * scores, axis=0, keepdims=True))
            halves.append(jnp.where(mine, grad_pair, 0.0))
        values_grad[:, lanes] = (
            split_product(jnp.concatenate(mixing, axis=1), jnp.concatenate(halves, axis=0))
            + weights[:, lanes] * arriving[:, lanes]
            + skip[:, lanes] * grad_pair
        )
    target_rows = jnp.concatenate(target_sums, axis=0)
    targets = exact_left(ones_where(row == column), target_rows, 3, 1, 1)
    writes_grad[...] = exact_right(scores_grad, read, 2) + split_product(
        weights * value, later, 1, 1
    )
    reads_grad[...] = exact_right(scores_grad, write, 2, 0, 0) + split_product(
        entered, before, 1, 1
    )
    inter = exact_right(entered * exact_left(read, before, 2), expand, 3, 1, 1)
    carried = exact_right(value * arriving, expand, 3, 1, 1)
    running_grad = targets + inter - source_sums * step - carried * weight
    state_sum = jnp.sum(later * before, axis=0, keepdims=True)
    state_heads = exact_right(jnp.broadcast_to(state_sum, (8, width)), expand, 3, 1, 1)[0:1]
    last = jnp.sum(carried * weight, axis=0, keepdims=True) + entry[length - 1 :] * state_heads
    logs_grad = exact_left(ones_where(row <= column), running_grad, 3) + last
    steps_grad[...] = source_sums + carried * to_end + logs_grad * rate[...]
    decay_grad[...] += jnp.sum(logs_grad * step * rate[...], axis=0, keepdims=True)
    skip_grad[...] += jnp.sum(grad * value, axis=0, keepdims=True)
    kept = exact_right(jnp.broadcast_to(entry[length - 1 :], (8, heads)), expand, 3)[0:1]
    adjoint[...] = kept * later + exact_left(read, entered, 2, 0, 0)


def scan_call(kernel, turns, reverse, operands, results, scratch, flops):
    def spec(shape, kind):
        def place(i):
            return turns - 1 - i if reverse else i

        if kind == "rows":
            return pl.BlockSpec((shape[0] // turns,) + shape[1:], lambda i: (place(i), 0))
        if kind == "columns":
            return pl.BlockSpec((shape[0], shape[1] // turns), lambda i: (0, place(i)))
        if kind == "turn":
            return pl.BlockSpec((1,) + shape[1:], lambda i: (place(i), 0, 0))
        return pl.BlockSpec(shape, lambda i: (0, 0))

    moved = sum(a.size * a.dtype.itemsize for a, _ in operands)
    return pl.pallas_call(
        kernel,
        grid=(turns,),
        in_specs=[spec(a.shape, kind) for a, kind in operands],
        out_specs=[spec(shape, kind) for shape, kind in results],
        out_shape=[jax.ShapeDtypeStruct(shape, jnp.float32) for shape, _ in results],
        scratch_shapes=[pltpu.VMEM(shape, jnp.float32) for shape in scratch],
        compiler_params=pltpu.CompilerParams(vmem_limit_bytes=40 * 1024 * 1024),
        cost_estimate=pl.CostEstimate(flops=flops, bytes_accessed=2 * moved, transcendentals=0),
    )(*[a for a, _ in operands])


def exchange_sum(blocks, axis):
    count = lax.axis_size(axis)
    place = lax.axis_index(axis)
    total = lax.dynamic_index_in_dim(blocks, place, 0, False).astype(jnp.float32)
    for hop in range(1, count):
        sent = lax.dynamic_index_in_dim(blocks, (place + hop) % count, 0, False)
        arrived = lax.ppermute(sent, axis, [(i, (i + hop) % count) for i in range(count)])
        total = total + arrived.astype(jnp.float32)
    return total


def exchange_rows(partial_sum, axis):
    count = lax.axis_size(axis)
    blocks = partial_sum.reshape((count, partial_sum.shape[0] // count) + partial_sum.shape[1:])
    return exchange_sum(blocks, axis)


def conv_apply(conv_in, rim, kernel, offset, valid):
    padded = jnp.concatenate([rim, conv_in], axis=0)
    group_rows = conv_in.shape[0]
    width = kernel.shape[0]
    total = offset[None, :]
    for tap_index in range(width):
        begin = width - 1 - tap_index
        total = total + kernel[tap_index][None, :] * jnp.where(
            valid[tap_index][:, None], padded[begin : begin + group_rows], 0.0
        )
    return jax.nn.silu(total)


def contract_last(left, right):
    return lax.dot_general(
        left, right, (((1,), (1,)), ((), ())), preferred_element_type=jnp.float32
    )


def contract_first(left, right):
    return lax.dot_general(
        left, right, (((0,), (0,)), ((), ())), preferred_element_type=jnp.float32
    )


def body(
    hidden_in,
    out_grad,
    seg_ids,
    norm_gain,
    gate_weight,
    value_weight,
    write_weight,
    read_weight,
    step_weight,
    step_bias,
    decay_log,
    skip_gain,
    conv_value,
    conv_write_read,
    conv_value_bias,
    conv_write_read_bias,
    gate_gain,
    out_weight,
):
    tensor_count = lax.axis_size("tensor")
    tensor_rank = lax.axis_index("tensor")
    data_rank = lax.axis_index("dp")
    own_rows = hidden_in.shape[0]
    group_rows = own_rows * tensor_count
    kernel_width = conv_value.shape[0]
    heads_here = step_weight.shape[1]
    inner_here = value_weight.shape[1]
    head_size = inner_here // heads_here
    state_here = write_weight.shape[1]
    state_size = state_here * tensor_count
    inner_total = inner_here * tensor_count
    gate_full, value_full, write_full, read_full, step_full, out_full = (
        lax.all_gather(gate_weight, "dp", axis=0, tiled=True),
        lax.all_gather(value_weight, "dp", axis=0, tiled=True),
        lax.all_gather(write_weight, "dp", axis=0, tiled=True),
        lax.all_gather(read_weight, "dp", axis=0, tiled=True),
        lax.all_gather(step_weight, "dp", axis=0, tiled=True),
        lax.all_gather(out_weight, "dp", axis=0, tiled=True),
    )
    hidden_rows, grad_rows = (
        lax.all_gather(hidden_in, "tensor", axis=0, tiled=True),
        lax.all_gather(out_grad, "tensor", axis=0, tiled=True),
    )
    hidden_float = hidden_rows.astype(jnp.float32)
    scale = lax.rsqrt(jnp.mean(hidden_float * hidden_float, axis=1, keepdims=True) + epsilon)
    normed = hidden_float * scale
    features = (normed * norm_gain[None, :]).astype(jnp.bfloat16)
    conv_full = jnp.concatenate([value_full, write_full, read_full], axis=1)
    gate_in = jnp.dot(features, gate_full, preferred_element_type=jnp.float32)
    conv_in = jnp.dot(features, conv_full, preferred_element_type=jnp.float32)
    step_in = jnp.dot(features, step_full, preferred_element_type=jnp.float32)
    rim = from_behind(conv_in[group_rows - (kernel_width - 1) :], "dp", 1)
    kernel = jnp.concatenate([conv_value, conv_write_read[0], conv_write_read[1]], axis=1)
    offset = jnp.concatenate([conv_value_bias, conv_write_read_bias[0], conv_write_read_bias[1]])
    padded_seg = jnp.concatenate([jnp.full((kernel_width - 1,), -1, jnp.int32), seg_ids])
    window = lax.dynamic_slice_in_dim(
        padded_seg, data_rank * group_rows, group_rows + kernel_width - 1
    )
    segment = window[kernel_width - 1 :]
    valid = jnp.stack(
        [
            window[kernel_width - 1 - tap_index : kernel_width - 1 - tap_index + group_rows]
            == segment
            for tap_index in range(kernel_width)
        ]
    )
    acted, conv_back = jax.vjp(partial(conv_apply, valid=valid), conv_in, rim, kernel, offset)
    values = acted[:, :inner_here]
    writes_low = acted[:, inner_here : inner_here + state_here].astype(jnp.bfloat16)
    reads_low = acted[:, inner_here + state_here :].astype(jnp.bfloat16)
    writes_all, reads_all = (
        lax.all_gather(writes_low, "tensor", axis=1, tiled=True),
        lax.all_gather(reads_low, "tensor", axis=1, tiled=True),
    )
    steps = jax.nn.softplus(step_in + step_bias[None, :])
    rate = -jnp.exp(decay_log)
    turns = group_rows // SPAN
    steps_row = steps.T
    rates = (rate[None, :], "whole"), (rate[:, None], "whole")
    seg_column = (segment[:, None], "rows")
    seg_line = (segment[None, :], "columns")
    before = window[kernel_width - 2 : kernel_width - 2 + group_rows][:, None]
    skip = (jnp.repeat(skip_gain, head_size)[None, :], "whole")
    state_shape = (state_size, inner_here)
    (state_end,) = scan_call(
        state_kernel,
        turns,
        False,
        [
            (values, "rows"),
            (writes_all, "rows"),
            (steps, "rows"),
            rates[0],
            seg_column,
            (before, "rows"),
        ],
        [(state_shape, "whole")],
        [],
        10**9,
    )
    state_in = from_behind(state_end, "dp", 1)
    shared = [
        (writes_all, "rows"),
        (reads_all, "rows"),
        (steps, "rows"),
        (steps_row, "columns"),
        *rates,
        seg_column,
        seg_line,
        (before, "rows"),
    ]
    mixed, states, entries = scan_call(
        forward_kernel,
        turns,
        False,
        [(values, "rows"), *shared, (before[:1], "whole"), skip, (state_in, "whole")],
        [
            (values.shape, "rows"),
            ((turns,) + state_shape, "turn"),
            (values.shape, "rows"),
        ],
        [state_shape, (1, heads_here)],
        10**10,
    )
    gate_act = jax.nn.silu(gate_in)
    gated = mixed * gate_act
    branch_grad = jnp.dot(grad_rows, out_full, preferred_element_type=jnp.float32)
    scaled = branch_grad * gate_gain[None, :]
    squares, dots = lax.psum(
        jnp.stack([jnp.sum(gated * gated, axis=1), jnp.sum(scaled * gated, axis=1)]), "tensor"
    )
    rms = lax.rsqrt(squares / inner_total + epsilon)
    branch = (gated * rms[:, None] * gate_gain[None, :]).astype(jnp.bfloat16)
    summed = exchange_rows(contract_last(branch, out_full).astype(jnp.bfloat16), "tensor")
    layer_out = hidden_in.astype(jnp.float32) + summed
    out_weight_grad = exchange_rows(contract_first(grad_rows, branch).astype(jnp.bfloat16), "dp")
    gate_gain_grad = jnp.sum(branch_grad * gated * rms[:, None], axis=0)
    gated_grad = rms[:, None] * scaled - gated * (rms * rms * rms * dots / inner_total)[:, None]
    mixed_grad = gated_grad * gate_act
    gate_sigmoid = jax.nn.sigmoid(gate_in)
    gate_grad = gated_grad * mixed * gate_sigmoid * (1.0 + gate_in * (1.0 - gate_sigmoid))
    carry_term = lax.dot_general(
        reads_all.astype(jnp.float32),
        entries * mixed_grad,
        (((0,), (0,)), ((), ())),
        precision=highest,
    )
    adjoint_in = from_behind(carry_term, "dp", -1)
    values_grad, writes_grad, reads_grad, steps_grad, decay_log_grad, skip_grad = scan_call(
        backward_kernel,
        turns,
        True,
        [
            (values, "rows"),
            (mixed_grad, "rows"),
            *shared,
            skip,
            (states, "turn"),
            (adjoint_in, "whole"),
        ],
        [
            (values.shape, "rows"),
            (writes_all.shape, "rows"),
            (writes_all.shape, "rows"),
            (steps.shape, "rows"),
            ((1, heads_here), "whole"),
            ((1, inner_here), "whole"),
        ],
        [state_shape],
        2 * 10**10,
    )
    decay_log_grad = decay_log_grad[0]
    skip_grad = jnp.sum(skip_grad.reshape(heads_here, head_size), axis=1)
    both = jnp.stack([writes_grad, reads_grad], axis=1).reshape(
        group_rows, 2, tensor_count, state_here
    )
    both = both.transpose(2, 0, 1, 3).reshape(tensor_count, group_rows, 2 * state_here)
    pair_part = exchange_sum(both, "tensor")
    acted_grad = jnp.concatenate([values_grad, pair_part], axis=1)
    conv_in_grad, rim_grad, kernel_grad, offset_grad = conv_back(acted_grad)
    rim_return = from_behind(rim_grad, "dp", -1)
    edge = group_rows - (kernel_width - 1)
    conv_in_grad = jnp.concatenate([conv_in_grad[:edge], conv_in_grad[edge:] + rim_return], axis=0)
    step_pre = steps_grad * jax.nn.sigmoid(step_in + step_bias[None, :])
    step_bias_grad = jnp.sum(step_pre, axis=0)
    gate_low = gate_grad.astype(jnp.bfloat16)
    conv_low = conv_in_grad.astype(jnp.bfloat16)
    step_low = step_pre.astype(jnp.bfloat16)
    features_grad = (
        contract_last(gate_low, gate_full)
        + contract_last(conv_low, conv_full)
        + contract_last(step_low, step_full)
    )
    gain_part = jnp.sum(features_grad * normed, axis=0)
    own_features_grad = exchange_rows(features_grad.astype(jnp.bfloat16), "tensor")
    norm_gain_grad = lax.psum_scatter(gain_part, "tensor", scatter_dimension=0, tiled=True)
    own_normed = lax.dynamic_slice_in_dim(normed, tensor_rank * own_rows, own_rows, 0)
    own_scale = lax.dynamic_slice_in_dim(scale, tensor_rank * own_rows, own_rows, 0)
    normed_grad = own_features_grad * norm_gain[None, :]
    input_grad = out_grad.astype(jnp.float32) + own_scale * (
        normed_grad - own_normed * jnp.mean(normed_grad * own_normed, axis=1, keepdims=True)
    )
    lows = jnp.concatenate([gate_low, conv_low, step_low], axis=1)
    joint = exchange_rows(contract_first(features, lows).astype(jnp.bfloat16), "dp")
    cuts = (inner_here, 2 * inner_here, 2 * inner_here + state_here, 2 * (inner_here + state_here))
    weight_sums = (*jnp.split(joint, cuts, axis=1), out_weight_grad)
    conv_value_grad = kernel_grad[:, :inner_here]
    conv_pair_grad = jnp.stack(
        [
            kernel_grad[:, inner_here : inner_here + state_here],
            kernel_grad[:, inner_here + state_here :],
        ]
    )
    conv_value_bias_grad = offset_grad[:inner_here]
    conv_pair_bias_grad = jnp.stack(
        [offset_grad[inner_here : inner_here + state_here], offset_grad[inner_here + state_here :]]
    )
    small = (
        norm_gain_grad,
        gate_gain_grad,
        step_bias_grad,
        decay_log_grad,
        skip_grad,
        conv_value_grad,
        conv_pair_grad,
        conv_value_bias_grad,
        conv_pair_bias_grad,
    )
    packed = lax.psum(jnp.concatenate([item.reshape(-1) for item in small]), "dp")
    small_sums = []
    begin = 0
    for item in small:
        small_sums.append(packed[begin : begin + item.size].reshape(item.shape))
        begin += item.size
    return (
        layer_out,
        input_grad,
        small_sums[0],
        weight_sums[0],
        weight_sums[1],
        weight_sums[2],
        weight_sums[3],
        weight_sums[4],
        small_sums[2],
        small_sums[3],
        small_sums[4],
        small_sums[5],
        small_sums[6],
        small_sums[7],
        small_sums[8],
        small_sums[1],
        weight_sums[5],
    )


def solution(mesh):
    return jax.shard_map(
        body,
        mesh=mesh,
        in_specs=(
            P(("dp", "tensor"), None),
            P(("dp", "tensor"), None),
            P(),
            P(),
            P("dp", "tensor"),
            P("dp", "tensor"),
            P("dp", "tensor"),
            P("dp", "tensor"),
            P("dp", "tensor"),
            P("tensor"),
            P("tensor"),
            P("tensor"),
            P(None, "tensor"),
            P(None, None, "tensor"),
            P("tensor"),
            P(None, "tensor"),
            P("tensor"),
            P("dp", "tensor"),
        ),
        out_specs=(
            P(("dp", "tensor"), None),
            P(("dp", "tensor"), None),
            P("tensor"),
            P("dp", "tensor"),
            P("dp", "tensor"),
            P("dp", "tensor"),
            P("dp", "tensor"),
            P("dp", "tensor"),
            P("tensor"),
            P("tensor"),
            P("tensor"),
            P(None, "tensor"),
            P(None, None, "tensor"),
            P("tensor"),
            P(None, "tensor"),
            P("tensor"),
            P("dp", "tensor"),
        ),
        check_vma=False,
    )
```

time: 1030 us -> 498 us (0.48)
  waiting for transfers between devices: 449 us -> 137 us
  matrix products: 151 us -> 35.7 us
  other arithmetic: 126 us -> 41.2 us
  local copies, waits for them, and re-layouts: 141 us -> 87.5 us
  Pallas kernels: 0 us -> 37.6 us
  starting transfers between devices: 5.47 us -> 39.9 us
  blocking collectives: 115 us -> 94.2 us
  loops' own time: 13.2 us -> 0 us
    reduce_scatter x10 -> x0, waiting for transfers between devices: 325 us -> none  [the longest x1 77.3 us: body(): lax.psum_scatter(features_grad, 'tensor', scatter_dimension=0, tiled=True)]
    dot_general x63 -> x1, matrix products: 108 us -> 1.65 us  [body(): lax.dot_general(reads_all.astype(jnp.float32), entries * mixed_grad, (((0...]
    ppermute x0 -> x23, waiting for transfers between devices: none -> 80.7 us  [exchange_sum(): lax.ppermute(sent, axis, [(i, (i + hop) % count) for i in range(count)])]
    all_gather x1, waiting for transfers between devices: 45.8 us -> 0.01 us  [body(): lax.all_gather(out_grad, 'tensor', axis=0, tiled=True)]
    pallas_call x0 -> x3, Pallas kernels: none -> 37.6 us  [scan_call(): pl.pallas_call(kernel, grid=(turns,), in_specs=[spec(a.shape, kind) for a...]
    ppermute x0 -> x23, starting transfers between devices: none -> 29.4 us  [exchange_sum(): lax.ppermute(sent, axis, [(i, (i + hop) % count) for i in range(count)])]
    another operation x80 -> x4, other arithmetic: 35.3 us -> 10.5 us
    another operation x46 -> x2, local copies, waits for them, and re-layouts: 24.5 us -> 0.75 us
  transfers between devices with their start and end apart: 19 -> 32, of which waited for: 16 -> 10; matrix products, arithmetic and copies ran while one was open for 17% -> 20% of each run, Pallas kernels for 0% -> 8%
where the time goes in v1:
time: 498 us; the launch traced here: 489 us
  waiting for transfers between devices  137 us (28%)
  blocking collectives  94.2 us (19%)
  local copies, waits for them, and re-layouts  87.5 us (18%)
  other arithmetic  41.2 us (8%)
  starting transfers between devices  39.9 us (8%)
  Pallas kernels  37.6 us (8%)
  matrix products  35.7 us (7%)
  between operations  16 us (3%)
    ppermute x23, waiting for transfers between devices, exchange_sum(): lax.ppermute(sent, axis, [(i, (i + hop) % count) for i in range(count)])  80.7 us
    pallas_call x3, Pallas kernels, scan_call(): pl.pallas_call(kernel, grid=(turns,), in_specs=[spec(a.shape, kind) for a...  37.6 us
    unnamed x164, local copies, waits for them, and re-layouts  32.9 us
    ppermute x23, starting transfers between devices, exchange_sum(): lax.ppermute(sent, axis, [(i, (i + hop) % count) for i in range(count)])  29.4 us
    all_gather x1, waiting for transfers between devices, body(): lax.all_gather(value_weight, 'dp', axis=0, tiled=True)  23.6 us
    psum x1, blocking collectives, body(): lax.psum(jnp.concatenate([item.reshape(-1) for item in small]), 'dp')  20.7 us
    all_gather x1, waiting for transfers between devices, body(): lax.all_gather(gate_weight, 'dp', axis=0, tiled=True)  17.2 us
    all_gather x1, blocking collectives, body(): lax.all_gather(reads_low, 'tensor', axis=1, tiled=True)  17 us
  transfers between devices with their start and end apart: 32, of which 10 were waited for; matrix products, arithmetic and copies ran while one was open for 20% of the time, Pallas kernels for 8%

profile of v1, /device:TPU:10, one launch (start us, length us, event | category | flops | bytes accessed | tf_op | source)
XLA Modules:
  0.0 488.6 jit_solution(644927054540020775)
XLA Ops:
  14.4 8.9 %all_gather.32 = bf16[1024,32]{0,1:T(8,128)(2,1)S(1)} all-gather(bf16[128,32]{0,1:T(8,128)(2,1)} %param.24), channel_id=1, replica_groups=mesh['dp'=8,'tensor'=4] {'dp'}, dimensions={0}, use_global_device_ids=true | all-gather | bytes 73728 | tf_op jit(solution)/shard_map/all_gather | solution.py:337
  23.5 8.1 %all_gather.33 = bf16[1024,32]{0,1:T(8,128)(2,1)S(1)} all-gather(bf16[128,32]{0,1:T(8,128)(2,1)} %param.25), channel_id=1, replica_groups=mesh['dp'=8,'tensor'=4] {'dp'}, dimensions={0}, use_global_device_ids=true | all-gather | bytes 73728 | tf_op jit(solution)/shard_map/all_gather | solution.py:338
  33.1 8.7 %all_gather.36 = bf16[1024,8]{0,1:T(8,128)(2,1)S(1)} all-gather(bf16[128,8]{0,1:T(8,128)(2,1)S(1)} %copy-done.65), channel_id=1, replica_groups=mesh['dp'=8,'tensor'=4] {'dp'}, dimensions={0}, use_global_device_ids=true | all-gather | bytes 18432 | tf_op jit(solution)/shard_map/all_gather | solution.py:339
  43.4 11.8 %all-gather.6.cloned.1.call-done = bf16[1024,1024]{1,0:T(8,128)(2,1)} async-done(((bf16[256,1024]{1,0:T(8,128)(2,1)}), bf16[1024,1024]{1,0:T(8,128)(2,1)}) %all-gather.6.cloned.1.call-update) | async-done | bytes 2097168 | tf_op jit(solution)/shard_map/all_gather | solution.py:343
  57.3 23.6 %all-gather.8.cloned.1.call-done = bf16[1024,512]{1,0:T(8,128)(2,1)} async-done(((bf16[128,512]{1,0:T(8,128)(2,1)}), bf16[1024,512]{1,0:T(8,128)(2,1)}) %all-gather.8.cloned.1.call-update) | async-done | bytes 1048592 | tf_op jit(solution)/shard_map/all_gather | solution.py:336
  89.1 17.2 %all-gather.10.cloned.1.call-done = bf16[1024,512]{1,0:T(8,128)(2,1)} async-done(((bf16[128,512]{1,0:T(8,128)(2,1)}), bf16[1024,512]{1,0:T(8,128)(2,1)}) %all-gather.10.cloned.1.call-update) | async-done | bytes 1048592 | tf_op jit(solution)/shard_map/all_gather | solution.py:335
  112.6 9.6 %fusion.59 = (bf16[1024,576]{1,0:T(8,128)(2,1)S(1)}, f32[1024,576]{1,0:T(8,128)}, f32[1024,576]{1,0:T(8,128)}) fusion(f32[1024,576]{1,0:T(8,128)} %copy-done.22, f32[3,576]{1,0:T(4,128)S(1)} %collective-permute-done, pred[1024]{0:T(1024)(128)(4,1)S(1)} %copy-done.58, f32[576]{0:T(1024)S(1)} %get-tuple-element.94, ...), kind=kLoop, calls=%fused_computation.170 | loop fusion | flops 11206656 | bytes 8279040 | tf_op jit(solution)/shard_map/convert.8
  123.2 14.5 %all_gather.34 = bf16[1024,128]{0,1:T(8,128)(2,1)S(1)} all-gather(bf16[1024,32]{0,1:T(8,128)(2,1)S(1)} %copy.119), channel_id=1, replica_groups=mesh['dp'=8,'tensor'=4] {'tensor'}, dimensions={1}, use_global_device_ids=true | all-gather | bytes 327680 | tf_op jit(solution)/shard_map/all_gather | solution.py:374
  140.7 6.9 %shard_map.305 = f32[128,512]{1,0:T(8,128)} custom-call(f32[1024,512]{1,0:T(8,128)S(1)} %slice.174.values, bf16[1024,128]{1,0:T(8,128)(2,1)S(1)} %copy.125.writes, f32[1024,8]{1,0:T(8,128)S(1)} %copy-done.2, f32[1,8]{1,0:T(1,128)S(1)} %get-tuple-element.169.rate, s32[1024,1]{1,0:T(8,128)S(1)} %copy.129.seg, s32[1024,1]{1,0:T(8,128)S(1)} %copy.130.seg_before), custom_call_target="tpu_custom_call" | custom-call | flops 1000000000 | bytes 4800576 | tf_op jit(solution)/shard_map/pallas_call | solution.py:248
  150.7 17.0 %all_gather.35 = bf16[1024,128]{0,1:T(8,128)(2,1)} all-gather(bf16[1024,32]{0,1:T(8,128)(2,1)S(1)} %copy.120), channel_id=1, replica_groups=mesh['dp'=8,'tensor'=4] {'tensor'}, dimensions={1}, use_global_device_ids=true | all-gather | bytes 327680 | tf_op jit(solution)/shard_map/all_gather | solution.py:375
  171.5 10.9 %shard_map.306 = (f32[1024,512]{1,0:T(8,128)S(1)}, f32[8,128,512]{2,1,0:T(8,128)S(1)}, f32[1024,512]{1,0:T(8,128)S(1)}) custom-call(f32[1024,512]{1,0:T(8,128)S(1)} %slice.174.values, bf16[1024,128]{1,0:T(8,128)(2,1)S(1)} %copy.125.writes, bf16[1024,128]{1,0:T(8,128)(2,1)S(1)} %copy-done.14, f32[1024,8]{1,0:T(8,128)S(1)} %copy-done.3, ...), custom_call_target="tpu_custom_call" | custom-call | flops 10000000000 | bytes 5927048 | tf_op jit(solution)/shard_map/pallas_call | solution.py:248
  186.4 6.8 %multiply_reduce_fusion.7 = (f32[1024]{0:T(1024)S(1)}, f32[1024]{0:T(1024)S(1)}, f32[1024,512]{1,0:T(8,128)}, f32[1024,512]{1,0:T(8,128)}) fusion(f32[512]{0:T(512)S(1)} %copy-done.64, f32[1024,512]{1,0:T(8,128)} %copy-done.9, f32[1024,512]{1,0:T(8,128)} %fusion.56, bf16[1024,1024]{1,0:T(8,128)(2,1)} %all-gather.12.cloned.1.call-done, ...), kind=kOutput, calls=%fused_computation.38 | convolution fusion | flops 1078982656 | bytes 11544576 | tf_op jit(solution)/shard_map/dot_general | solution.py:429
  193.2 9.2 %psum.14 = f32[2,1024]{1,0:T(2,128)S(1)} all-reduce(f32[2,1024]{1,0:T(2,128)S(1)} %pad_maximum_fusion.7), channel_id=1, replica_groups=mesh['dp'=8,'tensor'=4] {'tensor'}, use_global_device_ids=true, to_apply=%region_3.4 | all-reduce | flops 2048 | bytes 16384 | tf_op jit(solution)/shard_map/psum | solution.py:431
  222.6 5.2 %multiply_convert_fusion.1 = (bf16[1024,512]{1,0:T(8,128)(2,1)}, f32[1024,512]{1,0:T(8,128)S(1)}, f32[512]{0:T(512)S(1)}) fusion(f32[1024,512]{1,0:T(8,128)} %fusion.56, f32[1024,512]{1,0:T(8,128)} %copy-done.9, f32[1024,512]{1,0:T(8,128)} %get-tuple-element.98, f32[1024]{0:T(1024)S(1)} %fusion.44, f32[1024,512]{1,0:T(8,128)} %get-tuple-element.172, ...), kind=kLoop, calls=%fused_computation.34 | loop fusion | flops 9960960 | bytes 11546624 | tf_op jit(solution)/shard_map/convert_element_type | solution.py:488
  257.3 19.8 %shard_map.307 = (f32[1024,512]{1,0:T(8,128)S(1)}, f32[1024,128]{1,0:T(8,128)S(1)}, f32[1024,128]{1,0:T(8,128)S(1)}, f32[1024,8]{1,0:T(8,128)S(1)}, f32[1,8]{1,0:T(1,128)S(1)}, /*index=5*/f32[1,512]{1,0:T(1,128)S(1)}) custom-call(f32[1024,512]{1,0:T(8,128)S(1)} %slice.174.values, f32[1024,512]{1,0:T(8,128)S(1)} %copy-done.1, ...), custom_call_target="tpu_custom_call" | custom-call | flops 20000000000 | bytes 14315648 | tf_op jit(solution)/shard_map/pallas_call | solution.py:248
  295.6 22.8 %collective-permute-done.4 = bf16[256,1024]{1,0:T(8,128)(2,1)} collective-permute-done((bf16[256,1024]{1,0:T(8,128)(2,1)}, bf16[256,1024]{1,0:T(8,128)(2,1)}, u32[]{:S(2)}, u32[]{:S(2)}) %collective-permute-start.4) | collective-permute-done | bytes 524320 | tf_op jit(solution)/shard_map/ppermute | solution.py:266
  321.3 4.4 collective-permute-done.6
  325.7 10.5 %collective-permute-done.7 = f32[1024,64]{1,0:T(8,128)} collective-permute-done((f32[1024,64]{1,0:T(8,128)}, f32[1024,64]{1,0:T(8,128)}, u32[]{:S(2)}, u32[]{:S(2)}) %collective-permute-start.7) | collective-permute-done | bytes 262176 | tf_op jit(solution)/shard_map/ppermute | solution.py:266
  357.5 4.5 concatenate.37
  362.1 4.4 fusion.12
  367.2 5.5 %constant_dynamic-slice_fusion.15 = (bf16[1,128,1096]{1,0,2:T(2,128)(2,1)}, bf16[1,128,1096]{1,0,2:T(2,128)(2,1)}, bf16[1,128,1096]{1,0,2:T(2,128)(2,1)S(1)}, bf...) fusion(bf16[8,128,1096]{1,0,2:T(8,128)(2,1)S(1)} %bitcast.152, ...), kind=kLoop, calls=%fused_computation.131 | loop fusion | bytes 4489248 | tf_op jit(solution)/shard_map/jit(dynamic_index_in_dim)/dynamic_slice | solution.py:263
  386.1 7.2 %all-reduce.9 = f32[1024]{0:T(1024)S(1)} all-reduce(f32[1024]{0:T(1024)S(1)} %get-tuple-element.106), channel_id=2, replica_groups=mesh['dp'=8,'tensor'=4] {'tensor'}, use_global_device_ids=true, to_apply=%region_6.7.clone | all-reduce | flops 1024 | bytes 8192
  393.4 20.7 %psum.15 = f32[3672]{0:T(1024)S(1)} all-reduce(f32[3672]{0:T(1024)S(1)} %concatenate.36), channel_id=1, replica_groups=mesh['dp'=8,'tensor'=4] {'dp'}, use_global_device_ids=true, to_apply=%region_15.16 | all-reduce | flops 3672 | bytes 29376 | tf_op jit(solution)/shard_map/psum | solution.py:531
  441.6 30.9 %collective-permute-done.11 = bf16[256,1024]{1,0:T(8,128)(2,1)} collective-permute-done((bf16[256,1024]{1,0:T(8,128)(2,1)}, bf16[256,1024]{1,0:T(8,128)(2,1)}, u32[]{:S(2)}, u32[]{:S(2)}) %collective-permute-start.11) | collective-permute-done | bytes 524320 | tf_op jit(solution)/shard_map/ppermute | solution.py:266
  (332 shorter events, 183.4 us)
Async XLA Ops:
  7.3 47.9 %all-gather.6.cloned.1.call-start = ((), (), s32[]{:S(2)}) async-start(), calls=%async_computation | async-start | bytes 2621440 | tf_op jit(solution)/shard_map/all_gather | solution.py:343
  8.0 72.9 %all-gather.8.cloned.1.call-start = ((), (), s32[]{:S(2)}) async-start(), calls=%async_computation.1 | async-start | bytes 1179648 | tf_op jit(solution)/shard_map/all_gather | solution.py:336
  8.8 97.6 %all-gather.10.cloned.1.call-start = ((), (), s32[]{:S(2)}) async-start(), calls=%async_computation.2 | async-start | bytes 1179648 | tf_op jit(solution)/shard_map/all_gather | solution.py:335
  9.5 176.9 %all-gather.14.cloned.1.call-start = ((), (), s32[]{:S(2)}) async-start(), calls=%async_computation.4 | async-start | bytes 1179648 | tf_op jit(solution)/shard_map/all_gather | solution.py:340
  10.1 176.3 %all-gather.12.cloned.1.call-start = ((), (), s32[]{:S(2)}) async-start(), calls=%async_computation.3 | async-start | bytes 2621440 | tf_op jit(solution)/shard_map/all_gather | solution.py:344
  86.8 25.8 %collective-permute-start = (f32[3,576]{1,0:T(4,128)}, f32[3,576]{1,0:T(4,128)S(1)}, u32[]{:S(2)}, u32[]{:S(2)}) collective-permute-start(f32[3,576]{1,0:T(4,128)} %slice.167), channel_id=1, source_target_pairs={{0,4},{4,8},{8,12},{12,16},{16,20},{20,24},{24,28},{1,5},{5,9},{9,... | collective-permute-start | bytes 20744 | tf_op jit(solution)/shard_map/ppermute | solution.py:20
  147.6 21.8 %collective-permute-start.1 = (f32[128,512]{1,0:T(8,128)}, f32[128,512]{1,0:T(8,128)}, u32[]{:S(2)}, u32[]{:S(2)}) collective-permute-start(f32[128,512]{1,0:T(8,128)} %shard_map.305), channel_id=1, source_target_pairs={{0,4},{4,8},{8,12},{12,16},{16,20},{20,24},{24,28},{1,5},{5,9},{9,... | collective-permute-start | bytes 786440 | tf_op jit(solution)/shard_map/ppermute | solution.py:20
  211.3 24.2 %collective-permute-start.20 = (bf16[128,512]{1,0:T(8,128)(2,1)}, bf16[128,512]{1,0:T(8,128)(2,1)}, u32[]{:S(2)}, u32[]{:S(2)}) collective-permute-start(bf16[128,512]{1,0:T(8,128)(2,1)} %bitcast.170), channel_id=1, source_target_pairs={{0,4},{4,8},{8,12},{12,16},{16,20},{20,24},{24,28},{28,0},{1,5},{5... | collective-permute-start | bytes 393224 | tf_op jit(solution)/shard_map/ppermute | solution.py:266
  213.0 23.1 %collective-permute-start.21 = (bf16[128,512]{1,0:T(8,128)(2,1)}, bf16[128,512]{1,0:T(8,128)(2,1)}, u32[]{:S(2)}, u32[]{:S(2)}) collective-permute-start(bf16[128,512]{1,0:T(8,128)(2,1)} %bitcast.169), channel_id=1, source_target_pairs={{0,8},{4,12},{8,16},{12,20},{16,24},{20,28},{24,0},{28,4},{1,9},{5... | collective-permute-start | bytes 393224 | tf_op jit(solution)/shard_map/ppermute | solution.py:266
  219.5 24.5 %collective-permute-start.23 = (bf16[128,512]{1,0:T(8,128)(2,1)}, bf16[128,512]{1,0:T(8,128)(2,1)}, u32[]{:S(2)}, u32[]{:S(2)}) collective-permute-start(bf16[128,512]{1,0:T(8,128)(2,1)} %bitcast.166), channel_id=1, source_target_pairs={{0,16},{4,20},{8,24},{12,28},{16,0},{20,4},{24,8},{28,12},{1,17},{... | collective-permute-start | bytes 393224 | tf_op jit(solution)/shard_map/ppermute | solution.py:266
  222.5 23.2 %collective-permute-start.24 = (bf16[128,512]{1,0:T(8,128)(2,1)}, bf16[128,512]{1,0:T(8,128)(2,1)}, u32[]{:S(2)}, u32[]{:S(2)}) collective-permute-start(bf16[128,512]{1,0:T(8,128)(2,1)} %bitcast.165), channel_id=1, source_target_pairs={{0,20},{4,24},{8,28},{12,0},{16,4},{20,8},{24,12},{28,16},{1,21},{... | collective-permute-start | bytes 393224 | tf_op jit(solution)/shard_map/ppermute | solution.py:266
  244.0 51.4 %collective-permute-start.2 = (bf16[256,1024]{1,0:T(8,128)(2,1)}, bf16[256,1024]{1,0:T(8,128)(2,1)}, u32[]{:S(2)}, u32[]{:S(2)}) collective-permute-start(bf16[256,1024]{1,0:T(8,128)(2,1)} %get-tuple-element.127), channel_id=1, source_target_pairs={{0,1},{1,2},{2,3},{3,0},{4,5},{5,6},{6,7},{7,4},{8,9},{9,10},{10,1... | collective-permute-start | bytes 1572872 | tf_op jit(solution)/shard_map/ppermute | solution.py:266
  245.7 49.9 %collective-permute-start.3 = (bf16[256,1024]{1,0:T(8,128)(2,1)}, bf16[256,1024]{1,0:T(8,128)(2,1)}, u32[]{:S(2)}, u32[]{:S(2)}) collective-permute-start(bf16[256,1024]{1,0:T(8,128)(2,1)} %get-tuple-element.129), channel_id=1, source_target_pairs={{0,2},{1,3},{2,0},{3,1},{4,6},{5,7},{6,4},{7,5},{8,10},{9,11},{10,... | collective-permute-start | bytes 1572872 | tf_op jit(solution)/shard_map/ppermute | solution.py:266
  249.9 68.4 %collective-permute-start.4 = (bf16[256,1024]{1,0:T(8,128)(2,1)}, bf16[256,1024]{1,0:T(8,128)(2,1)}, u32[]{:S(2)}, u32[]{:S(2)}) collective-permute-start(bf16[256,1024]{1,0:T(8,128)(2,1)} %get-tuple-element.128), channel_id=1, source_target_pairs={{0,3},{1,0},{2,1},{3,2},{4,7},{5,4},{6,5},{7,6},{8,11},{9,8},{10,9... | collective-permute-start | bytes 1572872 | tf_op jit(solution)/shard_map/ppermute | solution.py:266
  284.6 41.2 %collective-permute-start.6 = (f32[1024,64]{1,0:T(8,128)}, f32[1024,64]{1,0:T(8,128)S(1)}, u32[]{:S(2)}, u32[]{:S(2)}) collective-permute-start(f32[1024,64]{1,0:T(8,128)} %bitcast.25), channel_id=1, source_target_pairs={{0,1},{1,2},{2,3},{3,0},{4,5},{5,6},{6,7},{7,4},{8,9},{9,10},{10,1... | collective-permute-start | bytes 786440 | tf_op jit(solution)/shard_map/ppermute | solution.py:266
  287.8 48.4 %collective-permute-start.7 = (f32[1024,64]{1,0:T(8,128)}, f32[1024,64]{1,0:T(8,128)}, u32[]{:S(2)}, u32[]{:S(2)}) collective-permute-start(f32[1024,64]{1,0:T(8,128)} %bitcast.26), channel_id=1, source_target_pairs={{0,2},{1,3},{2,0},{3,1},{4,6},{5,7},{6,4},{7,5},{8,10},{9,11},{10,... | collective-permute-start | bytes 786440 | tf_op jit(solution)/shard_map/ppermute | solution.py:266
  295.5 44.5 %collective-permute-start.8 = (f32[1024,64]{1,0:T(8,128)}, f32[1024,64]{1,0:T(8,128)S(1)}, u32[]{:S(2)}, u32[]{:S(2)}) collective-permute-start(f32[1024,64]{1,0:T(8,128)} %bitcast.162), channel_id=1, source_target_pairs={{0,3},{1,0},{2,1},{3,2},{4,7},{5,4},{6,5},{7,6},{8,11},{9,8},{10,9... | collective-permute-start | bytes 786440 | tf_op jit(solution)/shard_map/ppermute | solution.py:266
  373.4 44.8 %collective-permute-start.13 = (bf16[128,1096]{0,1:T(8,128)(2,1)}, bf16[128,1096]{0,1:T(8,128)(2,1)}, u32[]{:S(2)}, u32[]{:S(2)}) collective-permute-start(bf16[128,1096]{0,1:T(8,128)(2,1)} %bitcast.147), channel_id=1, source_target_pairs={{0,4},{4,8},{8,12},{12,16},{16,20},{20,24},{24,28},{28,0},{1,5},{5... | collective-permute-start | bytes 841736 | tf_op jit(solution)/shard_map/ppermute | solution.py:266
  374.2 47.2 %collective-permute-start.14 = (bf16[128,1096]{0,1:T(8,128)(2,1)}, bf16[128,1096]{0,1:T(8,128)(2,1)}, u32[]{:S(2)}, u32[]{:S(2)}) collective-permute-start(bf16[128,1096]{0,1:T(8,128)(2,1)} %bitcast.146), channel_id=1, source_target_pairs={{0,8},{4,12},{8,16},{12,20},{16,24},{20,28},{24,0},{28,4},{1,9},{5... | collective-permute-start | bytes 841736 | tf_op jit(solution)/shard_map/ppermute | solution.py:266
  376.1 49.3 %collective-permute-start.15 = (bf16[128,1096]{0,1:T(8,128)(2,1)}, bf16[128,1096]{0,1:T(8,128)(2,1)}, u32[]{:S(2)}, u32[]{:S(2)}) collective-permute-start(bf16[128,1096]{0,1:T(8,128)(2,1)} %bitcast.145), channel_id=1, source_target_pairs={{0,12},{4,16},{8,20},{12,24},{16,28},{20,0},{24,4},{28,8},{1,13},{... | collective-permute-start | bytes 841736 | tf_op jit(solution)/shard_map/ppermute | solution.py:266
  377.7 48.9 %collective-permute-start.16 = (bf16[128,1096]{0,1:T(8,128)(2,1)}, bf16[128,1096]{0,1:T(8,128)(2,1)}, u32[]{:S(2)}, u32[]{:S(2)}) collective-permute-start(bf16[128,1096]{0,1:T(8,128)(2,1)} %bitcast.144), channel_id=1, source_target_pairs={{0,16},{4,20},{8,24},{12,28},{16,0},{20,4},{24,8},{28,12},{1,17},{... | collective-permute-start | bytes 841736 | tf_op jit(solution)/shard_map/ppermute | solution.py:266
  379.4 51.5 %collective-permute-start.17 = (bf16[128,1096]{0,1:T(8,128)(2,1)S(1)}, bf16[128,1096]{0,1:T(8,128)(2,1)}, u32[]{:S(2)}, u32[]{:S(2)}) collective-permute-start(bf16[128,1096]{0,1:T(8,128)(2,1)S(1)} %bitcast.163), channel_id=1, source_target_pairs={{0,20},{4,24},{8,28},{12,0},{16,4},{20,8},{24,12},{28,16},{1,21},{... | collective-permute-start | bytes 841736 | tf_op jit(solution)/shard_map/ppermute | solution.py:266
  426.6 45.9 %collective-permute-start.11 = (bf16[256,1024]{1,0:T(8,128)(2,1)}, bf16[256,1024]{1,0:T(8,128)(2,1)}, u32[]{:S(2)}, u32[]{:S(2)}) collective-permute-start(bf16[256,1024]{1,0:T(8,128)(2,1)} %get-tuple-element.126), channel_id=1, source_target_pairs={{0,2},{1,3},{2,0},{3,1},{4,6},{5,7},{6,4},{7,5},{8,10},{9,11},{10,... | collective-permute-start | bytes 1572872 | tf_op jit(solution)/shard_map/ppermute | solution.py:266
  430.8 45.5 %collective-permute-start.12 = (bf16[256,1024]{1,0:T(8,128)(2,1)}, bf16[256,1024]{1,0:T(8,128)(2,1)}, u32[]{:S(2)}, u32[]{:S(2)}) collective-permute-start(bf16[256,1024]{1,0:T(8,128)(2,1)} %get-tuple-element.125), channel_id=1, source_target_pairs={{0,3},{1,0},{2,1},{3,2},{4,7},{5,4},{6,5},{7,6},{8,11},{9,8},{10,9... | collective-permute-start | bytes 1572872 | tf_op jit(solution)/shard_map/ppermute | solution.py:266
  (83 other events, 1668.8 us)
Sparse Core Ops, SparseCore 0:
  9.7 45.4 all-gather.5
  57.1 23.7 all-gather.7
  82.8 23.4 all-gather.9
  108.1 23.4 all-gather.13
  133.0 48.6 all-gather.11

commit v2 on v1

--- a/solution.py
+++ b/solution.py
@@ -79,7 +79,15 @@
     return running, entry, to_end
 
 
-def state_kernel(values, writes, steps, rate, seg, seg_before, state):
+def joined(pairs, second):
+    count, _, width = pairs.shape
+    begin = width // 2 if second else 0
+    return jnp.concatenate(
+        [pairs[i, :, begin : begin + width // 2] for i in range(count)], axis=1
+    )
+
+
+def state_kernel(values, pairs, steps, rate, seg, seg_before, state):
     length, width = values.shape
     heads = steps.shape[1]
 
@@ -93,11 +101,11 @@
     _, entry, to_end = decays(row, column, step, rate[...], seg[...], seg_before[...])
     weighted = exact_right(to_end * step, expand, 3) * values[...]
     kept = exact_right(jnp.broadcast_to(entry[length - 1 :], (8, heads)), expand, 3)[0:1]
-    state[...] = kept * state[...] + exact_left(writes[...], weighted, 2, 0, 0)
+    state[...] = kept * state[...] + exact_left(joined(pairs, False), weighted, 2, 0, 0)
 
 
 def forward_kernel(
-    values, writes, reads, steps, steps_row, rate, rate_row, seg, seg_row, seg_before, seg_group,
+    values, pairs, steps, steps_row, rate, rate_row, seg, seg_row, seg_before, seg_group,
     skip, state_in, mixed, states, entries, state, total,
 ):
     length, width = values.shape
@@ -116,10 +124,11 @@
     running, entry, to_end = decays(row, column, step, rate[...], seg[...], seg_before[...])
     running_row = exact_right(step_row * rate_row[...], ones_where(row <= column), 3)
     same = (seg[...] == seg_row[...]) & (row >= column)
-    scores = product(reads[...], writes[...], 1, 1)
+    write, read = joined(pairs, False), joined(pairs, True)
+    scores = product(read, write, 1, 1)
     before = state[...]
     states[0] = before
-    outer = exact_right(entry, expand, 3) * exact_left(reads[...], before, 2)
+    outer = exact_right(entry, expand, 3) * exact_left(read, before, 2)
     lane = lax.broadcasted_iota(jnp.int32, (length, pair), 1)
     for j in range(heads // 2):
         lanes = slice(j * pair, (j + 1) * pair)
@@ -141,7 +150,7 @@
         )
     weighted = exact_right(to_end * step, expand, 3) * values[...]
     kept = exact_right(jnp.broadcast_to(entry[length - 1 :], (8, heads)), expand, 3)[0:1]
-    state[...] = kept * before + exact_left(writes[...], weighted, 2, 0, 0)
+    state[...] = kept * before + exact_left(write, weighted, 2, 0, 0)
     whole = total[...] + running
     total[...] = whole[length - 1 :]
     entries[...] = exact_right(
@@ -150,8 +159,8 @@
 
 
 def backward_kernel(
-    values, grads, writes, reads, steps, steps_row, rate, rate_row, seg, seg_row, seg_before,
-    skip, states, adjoint_in, values_grad, writes_grad, reads_grad, steps_grad, decay_grad,
+    values, grads, pairs, steps, steps_row, rate, rate_row, seg, seg_row, seg_before,
+    skip, states, adjoint_in, values_grad, pairs_grad, steps_grad, decay_grad,
     skip_grad, adjoint,
 ):
     length, width = values.shape
@@ -170,8 +179,7 @@
     running, entry, to_end = decays(row, column, step, rate[...], seg[...], seg_before[...])
     running_row = exact_right(steps_row[...] * rate_row[...], ones_where(row <= column), 3)
     same = (seg[...] == seg_row[...]) & (row <= column)
-    write = writes[...]
-    read = reads[...]
+    write, read = joined(pairs, False), joined(pairs, True)
     scores = product(write, read, 1, 1)
     later = adjoint[...]
     before = states[0]
@@ -211,12 +219,16 @@
         )
     target_rows = jnp.concatenate(target_sums, axis=0)
     targets = exact_left(ones_where(row == column), target_rows, 3, 1, 1)
-    writes_grad[...] = exact_right(scores_grad, read, 2) + split_product(
+    writes_grad = exact_right(scores_grad, read, 2) + split_product(
         weights * value, later, 1, 1
     )
-    reads_grad[...] = exact_right(scores_grad, write, 2, 0, 0) + split_product(
+    reads_grad = exact_right(scores_grad, write, 2, 0, 0) + split_product(
         entered, before, 1, 1
     )
+    share = pairs.shape[2] // 2
+    for i in range(pairs.shape[0]):
+        mine = slice(i * share, (i + 1) * share)
+        pairs_grad[i] = jnp.concatenate([writes_grad[:, mine], reads_grad[:, mine]], axis=1)
     inter = exact_right(entered * exact_left(read, before, 2), expand, 3, 1, 1)
     carried = exact_right(value * arriving, expand, 3, 1, 1)
     running_grad = targets + inter - source_sums * step - carried * weight
@@ -240,6 +252,10 @@
             return pl.BlockSpec((shape[0] // turns,) + shape[1:], lambda i: (place(i), 0))
         if kind == "columns":
             return pl.BlockSpec((shape[0], shape[1] // turns), lambda i: (0, place(i)))
+        if kind == "parts":
+            return pl.BlockSpec(
+                (shape[0], shape[1] // turns, shape[2]), lambda i: (0, place(i), 0)
+            )
         if kind == "turn":
             return pl.BlockSpec((1,) + shape[1:], lambda i: (place(i), 0, 0))
         return pl.BlockSpec(shape, lambda i: (0, 0))
@@ -272,6 +288,80 @@
     count = lax.axis_size(axis)
     blocks = partial_sum.reshape((count, partial_sum.shape[0] // count) + partial_sum.shape[1:])
     return exchange_sum(blocks, axis)
+
+
+def transfer_kernel(plan, *refs):
+    count = len(plan)
+    sources, targets = refs[:count], refs[count : 2 * count]
+    send, receive, local = refs[2 * count :]
+    axes = sorted({axis for axis, _ in plan})
+    barrier = pltpu.get_barrier_semaphore()
+    for axis in axes:
+        size = lax.axis_size(axis)
+        for hop in range(1, size):
+            peer = lax.rem(lax.axis_index(axis) + hop, size)
+            pl.semaphore_signal(
+                barrier, inc=1, device_id={axis: peer}, device_id_type=pl.DeviceIdType.MESH
+            )
+    pl.semaphore_wait(barrier, sum(lax.axis_size(axis) - 1 for axis in axes))
+    copies = []
+    slot = 0
+    for item, (axis, blocks) in enumerate(plan):
+        size = lax.axis_size(axis)
+        me = lax.axis_index(axis)
+        for hop in range(1, size):
+            peer = lax.rem(me + hop, size)
+            copy = pltpu.make_async_remote_copy(
+                src_ref=sources[item].at[peer] if blocks else sources[item],
+                dst_ref=targets[item].at[me],
+                send_sem=send.at[slot],
+                recv_sem=receive.at[slot],
+                device_id={axis: peer},
+                device_id_type=pl.DeviceIdType.MESH,
+            )
+            copy.start()
+            copies.append(copy)
+            slot += 1
+        own = pltpu.make_async_copy(
+            sources[item].at[me] if blocks else sources[item], targets[item].at[me], local.at[item]
+        )
+        own.start()
+        copies.append(own)
+    for copy in copies:
+        copy.wait()
+
+
+def transfer(items, number):
+    plan = tuple((axis, blocks) for _, axis, blocks in items)
+    shapes = []
+    slots = 0
+    for array, axis, blocks in items:
+        size = lax.axis_size(axis)
+        shapes.append(
+            jax.ShapeDtypeStruct(array.shape if blocks else (size,) + array.shape, array.dtype)
+        )
+        slots += size - 1
+    return pl.pallas_call(
+        partial(transfer_kernel, plan),
+        in_specs=[pl.BlockSpec(memory_space=pl.ANY)] * len(items),
+        out_specs=[pl.BlockSpec(memory_space=pl.ANY)] * len(items),
+        out_shape=shapes,
+        scratch_shapes=[
+            pltpu.SemaphoreType.DMA((slots,)),
+            pltpu.SemaphoreType.DMA((slots,)),
+            pltpu.SemaphoreType.DMA((len(items),)),
+        ],
+        compiler_params=pltpu.CompilerParams(collective_id=number, has_side_effects=True),
+    )(*[array for array, _, _ in items])
+
+
+def blocks_of(array, axis):
+    count = lax.axis_size(axis)
+    return array.reshape((count, array.shape[0] // count) + array.shape[1:])
+
+
+def total_of(arrived):
+    return jnp.sum(arrived.astype(jnp.float32), axis=0)
 
 
 def conv_apply(conv_in, rim, kernel, offset, valid):
@@ -331,29 +421,42 @@
     state_here = write_weight.shape[1]
     state_size = state_here * tensor_count
     inner_total = inner_here * tensor_count
-    gate_full, value_full, write_full, read_full, step_full, out_full = (
-        lax.all_gather(gate_weight, "dp", axis=0, tiled=True),
-        lax.all_gather(value_weight, "dp", axis=0, tiled=True),
-        lax.all_gather(write_weight, "dp", axis=0, tiled=True),
-        lax.all_gather(read_weight, "dp", axis=0, tiled=True),
-        lax.all_gather(step_weight, "dp", axis=0, tiled=True),
-        lax.all_gather(out_weight, "dp", axis=0, tiled=True),
-    )
-    hidden_rows, grad_rows = (
-        lax.all_gather(hidden_in, "tensor", axis=0, tiled=True),
-        lax.all_gather(out_grad, "tensor", axis=0, tiled=True),
-    )
+    gate_full, value_full, rest_full, hidden_rows = transfer(
+        [
+            (gate_weight, "dp", False),
+            (value_weight, "dp", False),
+            (jnp.concatenate([write_weight, read_weight, step_weight], axis=1), "dp", False),
+            (hidden_in, "tensor", False),
+        ],
+        1,
+    )
+    gate_full, value_full, rest_full, hidden_rows = (
+        item.reshape((-1, item.shape[2]))
+        for item in (gate_full, value_full, rest_full, hidden_rows)
+    )
+    grad_source, out_source, hidden_rows = lax.optimization_barrier(
+        (out_grad, out_weight, hidden_rows)
+    )
+    grad_rows = lax.all_gather(grad_source, "tensor", axis=0, tiled=True)
+    out_full = lax.all_gather(out_source, "dp", axis=0, tiled=True)
     hidden_float = hidden_rows.astype(jnp.float32)
     scale = lax.rsqrt(jnp.mean(hidden_float * hidden_float, axis=1, keepdims=True) + epsilon)
     normed = hidden_float * scale
     features = (normed * norm_gain[None, :]).astype(jnp.bfloat16)
-    conv_full = jnp.concatenate([value_full, write_full, read_full], axis=1)
     gate_in = jnp.dot(features, gate_full, preferred_element_type=jnp.float32)
-    conv_in = jnp.dot(features, conv_full, preferred_element_type=jnp.float32)
-    step_in = jnp.dot(features, step_full, preferred_element_type=jnp.float32)
-    rim = from_behind(conv_in[group_rows - (kernel_width - 1) :], "dp", 1)
-    kernel = jnp.concatenate([conv_value, conv_write_read[0], conv_write_read[1]], axis=1)
-    offset = jnp.concatenate([conv_value_bias, conv_write_read_bias[0], conv_write_read_bias[1]])
+    value_in = jnp.dot(features, value_full, preferred_element_type=jnp.float32)
+    rest_in = jnp.dot(features, rest_full, preferred_element_type=jnp.float32)
+    pair_in, step_in = rest_in[:, : 2 * state_here], rest_in[:, 2 * state_here :]
+    rim = from_behind(
+        jnp.concatenate(
+            [item[group_rows - (kernel_width - 1) :] for item in (value_in, pair_in)], axis=1
+        ),
+        "dp",
+        1,
+    )
+    value_rim, pair_rim = rim[:, :inner_here], rim[:, inner_here:]
+    pair_kernel = jnp.concatenate([conv_write_read[0], conv_write_read[1]], axis=1)
+    pair_offset = conv_write_read_bias.reshape(-1)
     padded_seg = jnp.concatenate([jnp.full((kernel_width - 1,), -1, jnp.int32), seg_ids])
     window = lax.dynamic_slice_in_dim(
         padded_seg, data_rank * group_rows, group_rows + kernel_width - 1
@@ -366,14 +469,10 @@
             for tap_index in range(kernel_width)
         ]
     )
-    acted, conv_back = jax.vjp(partial(conv_apply, valid=valid), conv_in, rim, kernel, offset)
-    values = acted[:, :inner_here]
-    writes_low = acted[:, inner_here : inner_here + state_here].astype(jnp.bfloat16)
-    reads_low = acted[:, inner_here + state_here :].astype(jnp.bfloat16)
-    writes_all, reads_all = (
-        lax.all_gather(writes_low, "tensor", axis=1, tiled=True),
-        lax.all_gather(reads_low, "tensor", axis=1, tiled=True),
-    )
+    convolve = partial(conv_apply, valid=valid)
+    pair, pair_back = jax.vjp(convolve, pair_in, pair_rim, pair_kernel, pair_offset)
+    values, value_back = jax.vjp(convolve, value_in, value_rim, conv_value, conv_value_bias)
+    (pairs,) = transfer([(pair.astype(jnp.bfloat16), "tensor", False)], 2)
     steps = jax.nn.softplus(step_in + step_bias[None, :])
     rate = -jnp.exp(decay_log)
     turns = group_rows // SPAN
@@ -390,7 +489,7 @@
         False,
         [
             (values, "rows"),
-            (writes_all, "rows"),
+            (pairs, "parts"),
             (steps, "rows"),
             rates[0],
             seg_column,
@@ -402,8 +501,7 @@
     )
     state_in = from_behind(state_end, "dp", 1)
     shared = [
-        (writes_all, "rows"),
-        (reads_all, "rows"),
+        (pairs, "parts"),
         (steps, "rows"),
         (steps_row, "columns"),
         *rates,
@@ -428,9 +526,17 @@
     gated = mixed * gate_act
     branch_grad = jnp.dot(grad_rows, out_full, preferred_element_type=jnp.float32)
     scaled = branch_grad * gate_gain[None, :]
-    squares, dots = lax.psum(
-        jnp.stack([jnp.sum(gated * gated, axis=1), jnp.sum(scaled * gated, axis=1)]), "tensor"
-    )
+    (token_sums,) = transfer(
+        [
+            (
+                jnp.stack([jnp.sum(gated * gated, axis=1), jnp.sum(scaled * gated, axis=1)]),
+                "tensor",
+                False,
+            )
+        ],
+        3,
+    )
+    squares, dots = total_of(token_sums)
     rms = lax.rsqrt(squares / inner_total + epsilon)
     branch = (gated * rms[:, None] * gate_gain[None, :]).astype(jnp.bfloat16)
     summed = exchange_rows(contract_last(branch, out_full).astype(jnp.bfloat16), "tensor")
@@ -442,13 +548,13 @@
     gate_sigmoid = jax.nn.sigmoid(gate_in)
     gate_grad = gated_grad * mixed * gate_sigmoid * (1.0 + gate_in * (1.0 - gate_sigmoid))
     carry_term = lax.dot_general(
-        reads_all.astype(jnp.float32),
+        pairs[:, :, state_here:].transpose(1, 0, 2).reshape(group_rows, state_size).astype(jnp.float32),
         entries * mixed_grad,
         (((0,), (0,)), ((), ())),
         precision=highest,
     )
     adjoint_in = from_behind(carry_term, "dp", -1)
-    values_grad, writes_grad, reads_grad, steps_grad, decay_log_grad, skip_grad = scan_call(
+    values_grad, pairs_grad, steps_grad, decay_log_grad, skip_grad = scan_call(
         backward_kernel,
         turns,
         True,
@@ -462,8 +568,7 @@
         ],
         [
             (values.shape, "rows"),
-            (writes_all.shape, "rows"),
-            (writes_all.shape, "rows"),
+            (pairs.shape, "parts"),
             (steps.shape, "rows"),
             ((1, heads_here), "whole"),
             ((1, inner_here), "whole"),
@@ -473,71 +578,85 @@
     )
     decay_log_grad = decay_log_grad[0]
     skip_grad = jnp.sum(skip_grad.reshape(heads_here, head_size), axis=1)
-    both = jnp.stack([writes_grad, reads_grad], axis=1).reshape(
-        group_rows, 2, tensor_count, state_here
-    )
-    both = both.transpose(2, 0, 1, 3).reshape(tensor_count, group_rows, 2 * state_here)
-    pair_part = exchange_sum(both, "tensor")
-    acted_grad = jnp.concatenate([values_grad, pair_part], axis=1)
-    conv_in_grad, rim_grad, kernel_grad, offset_grad = conv_back(acted_grad)
-    rim_return = from_behind(rim_grad, "dp", -1)
+    pair_grad = exchange_sum(pairs_grad, "tensor")
+    value_in_grad, value_rim_grad, value_kernel_grad, value_offset_grad = value_back(values_grad)
+    pair_in_grad, pair_rim_grad, pair_kernel_grad, pair_offset_grad = pair_back(pair_grad)
     edge = group_rows - (kernel_width - 1)
-    conv_in_grad = jnp.concatenate([conv_in_grad[:edge], conv_in_grad[edge:] + rim_return], axis=0)
+    value_in_grad = value_in_grad.at[edge:].add(from_behind(value_rim_grad, "dp", -1))
+    pair_in_grad = pair_in_grad.at[edge:].add(from_behind(pair_rim_grad, "dp", -1))
     step_pre = steps_grad * jax.nn.sigmoid(step_in + step_bias[None, :])
     step_bias_grad = jnp.sum(step_pre, axis=0)
     gate_low = gate_grad.astype(jnp.bfloat16)
-    conv_low = conv_in_grad.astype(jnp.bfloat16)
-    step_low = step_pre.astype(jnp.bfloat16)
+    value_low = value_in_grad.astype(jnp.bfloat16)
+    rest_low = jnp.concatenate([pair_in_grad, step_pre], axis=1).astype(jnp.bfloat16)
     features_grad = (
         contract_last(gate_low, gate_full)
-        + contract_last(conv_low, conv_full)
-        + contract_last(step_low, step_full)
+        + contract_last(value_low, value_full)
+        + contract_last(rest_low, rest_full)
     )
     gain_part = jnp.sum(features_grad * normed, axis=0)
-    own_features_grad = exchange_rows(features_grad.astype(jnp.bfloat16), "tensor")
-    norm_gain_grad = lax.psum_scatter(gain_part, "tensor", scatter_dimension=0, tiled=True)
+    gate_share, value_share, rest_share = (
+        blocks_of(contract_first(features, low).astype(jnp.bfloat16), "dp")
+        for low in (gate_low, value_low, rest_low)
+    )
+    small = (
+        gain_part,
+        gate_gain_grad,
+        step_bias_grad,
+        decay_log_grad,
+        skip_grad,
+        value_kernel_grad,
+        pair_kernel_grad,
+        value_offset_grad,
+        pair_offset_grad,
+    )
+    flat = jnp.concatenate([item.reshape(-1) for item in small])
+    flat = jnp.pad(flat, (0, -flat.size % 1024)).reshape(-1, 128)
+    features_parts, gate_parts, value_parts, rest_parts, flat_parts = transfer(
+        [
+            (blocks_of(features_grad.astype(jnp.bfloat16), "tensor"), "tensor", True),
+            (gate_share, "dp", True),
+            (value_share, "dp", True),
+            (rest_share, "dp", True),
+            (flat, "dp", False),
+        ],
+        4,
+    )
+    own_features_grad = total_of(features_parts)
+    packed = total_of(flat_parts).reshape(-1)
+    small_sums = []
+    begin = 0
+    for item in small:
+        small_sums.append(packed[begin : begin + item.size].reshape(item.shape))
+        begin += item.size
+    (gain_parts,) = transfer(
+        [(small_sums[0].reshape(tensor_count, 1, -1), "tensor", True)],
+        5,
+    )
+    norm_gain_grad = total_of(gain_parts)[0]
     own_normed = lax.dynamic_slice_in_dim(normed, tensor_rank * own_rows, own_rows, 0)
     own_scale = lax.dynamic_slice_in_dim(scale, tensor_rank * own_rows, own_rows, 0)
     normed_grad = own_features_grad * norm_gain[None, :]
     input_grad = out_grad.astype(jnp.float32) + own_scale * (
         normed_grad - own_normed * jnp.mean(normed_grad * own_normed, axis=1, keepdims=True)
     )
-    lows = jnp.concatenate([gate_low, conv_low, step_low], axis=1)
-    joint = exchange_rows(contract_first(features, lows).astype(jnp.bfloat16), "dp")
-    cuts = (inner_here, 2 * inner_here, 2 * inner_here + state_here, 2 * (inner_here + state_here))
-    weight_sums = (*jnp.split(joint, cuts, axis=1), out_weight_grad)
-    conv_value_grad = kernel_grad[:, :inner_here]
-    conv_pair_grad = jnp.stack(
-        [
-            kernel_grad[:, inner_here : inner_here + state_here],
-            kernel_grad[:, inner_here + state_here :],
-        ]
-    )
-    conv_value_bias_grad = offset_grad[:inner_here]
-    conv_pair_bias_grad = jnp.stack(
-        [offset_grad[inner_here : inner_here + state_here], offset_grad[inner_here + state_here :]]
-    )
-    small = (
-        norm_gain_grad,
-        gate_gain_grad,
-        step_bias_grad,
-        decay_log_grad,
-        skip_grad,
-        conv_value_grad,
-        conv_pair_grad,
-        conv_value_bias_grad,
-        conv_pair_bias_grad,
-    )
-    packed = lax.psum(jnp.concatenate([item.reshape(-1) for item in small]), "dp")
-    small_sums = []
-    begin = 0
-    for item in small:
-        small_sums.append(packed[begin : begin + item.size].reshape(item.shape))
-        begin += item.size
+    rest_sum = total_of(rest_parts)
+    weight_sums = (
+        total_of(gate_parts),
+        total_of(value_parts),
+        rest_sum[:, :state_here],
+        rest_sum[:, state_here : 2 * state_here],
+        rest_sum[:, 2 * state_here :],
+        out_weight_grad,
+    )
+
+    def paired(array):
+        return jnp.stack([array[..., :state_here], array[..., state_here:]])
+
     return (
         layer_out,
         input_grad,
-        small_sums[0],
+        norm_gain_grad,
         weight_sums[0],
         weight_sums[1],
         weight_sums[2],
@@ -547,9 +666,9 @@
         small_sums[3],
         small_sums[4],
         small_sums[5],
-        small_sums[6],
+        paired(small_sums[6]),
         small_sums[7],
-        small_sums[8],
+        paired(small_sums[8]),
         small_sums[1],
         weight_sums[5],
     )

time: 498 us -> 406 us (0.82); the launches traced: 489 us -> 403 us
  Pallas kernels: 37.6 us -> 195 us
  waiting for transfers between devices: 137 us -> 41.9 us
  blocking collectives: 94.2 us -> 0 us
  local copies, waits for them, and re-layouts: 87.5 us -> 38.3 us
  starting transfers between devices: 39.9 us -> 31.8 us
  other arithmetic: 41.2 us -> 46.9 us
    pallas_call x0 -> x5, Pallas kernels: none -> 158 us  [transfer(): pl.pallas_call(partial(transfer_kernel, plan), in_specs=[pl.BlockSpec(mem...]
    all_gather x5 -> x0, blocking collectives: 57.2 us -> none  [the longest x1 17 us: body(): lax.all_gather(reads_low, 'tensor', axis=1, tiled=True)]
    all_gather x5 -> x2, waiting for transfers between devices: 52.7 us -> 0.01 us  [the longest x1 0.01 us: body(): out_full = lax.all_gather(out_source, 'dp', axis=0, tiled=True)]
    ppermute x23 -> x13, waiting for transfers between devices: 80.7 us -> 41.3 us  [exchange_sum(): lax.ppermute(sent, axis, [(i, (i + hop) % count) for i in range(count)])]
    psum x2 -> x0, blocking collectives: 29.9 us -> none  [the longest x1 20.7 us: body(): lax.psum(jnp.concatenate([item.reshape(-1) for item in small]), 'dp')]
    dynamic_slice x14 -> x0, local copies, waits for them, and re-layouts: 24.1 us -> none  [the longest x10 15.1 us: exchange_sum(): sent = lax.dynamic_index_in_dim(blocks, (place + hop) % count, 0, False)]
    unnamed x164 -> x123, local copies, waits for them, and re-layouts: 32.9 us -> 17.4 us
    ppermute x23 -> x13, starting transfers between devices: 29.4 us -> 15.7 us  [exchange_sum(): lax.ppermute(sent, axis, [(i, (i + hop) % count) for i in range(count)])]
  transfers between devices with their start and end apart: 32 -> 20, of which waited for: 10 -> 3; matrix products, arithmetic and copies ran while one was open for 20% -> 14% of each run, Pallas kernels for 8% -> 21%
where the time goes in v2:
time: 406 us; the launch traced here: 403 us
  Pallas kernels  195 us (48%)
  other arithmetic  46.9 us (12%)
  waiting for transfers between devices  41.9 us (10%)
  local copies, waits for them, and re-layouts  38.3 us (9%)
  matrix products  34.5 us (8%)
  starting transfers between devices  31.8 us (8%)
  between operations  15 us (4%)
    pallas_call x5, Pallas kernels, transfer(): pl.pallas_call(partial(transfer_kernel, plan), in_specs=[pl.BlockSpec(mem...  158 us
    ppermute x13, waiting for transfers between devices, exchange_sum(): lax.ppermute(sent, axis, [(i, (i + hop) % count) for i in range(count)])  41.3 us
    pallas_call x3, Pallas kernels, scan_call(): pl.pallas_call(kernel, grid=(turns,), in_specs=[spec(a.shape, kind) for a...  36.8 us
    unnamed x123, local copies, waits for them, and re-layouts  17.4 us
    ppermute x5, starting transfers between devices, from_behind(): lax.ppermute(value, axis, [(source, source + steps) for source in range(l...  16 us
    ppermute x13, starting transfers between devices, exchange_sum(): lax.ppermute(sent, axis, [(i, (i + hop) % count) for i in range(count)])  15.7 us
    dot_general x4, matrix products, contract_last(): lax.dot_general(left, right, (((1,), (1,)), ((), ())), preferred_element_...  10.8 us
    dot_general x4, matrix products, contract_first(): lax.dot_general(left, right, (((0,), (0,)), ((), ())), preferred_element_...  8.9 us
  transfers between devices with their start and end apart: 20, of which 3 were waited for; matrix products, arithmetic and copies ran while one was open for 14% of the time, Pallas kernels for 21%

profile of v2, /device:TPU:10, one launch (start us, length us, event | category | flops | bytes accessed | tf_op | source)
XLA Modules:
  0.0 403.2 jit_solution(6246210458525651936)
XLA Ops:
  10.4 50.0 %shard_map.305 = (bf16[8,128,512]{2,1,0:T(8,128)(2,1)}, bf16[8,128,512]{2,1,0:T(8,128)(2,1)}, bf16[8,128,72]{2,1,0:T(8,128)(2,1)}, bf16[4,256,1024]{2,1,0:T(8,128)(2,1)}) custom-call(bf16[128,512]{1,0:T(8,128)(2,1)} %refs_0_.1, bf16[128,512]{1,0:T(8,128)(2,1)} %refs_1_.1, bf16[128,72]{1,0:T(8,128)(2,1)} %pad_maximum_fusion.5.refs_2_, bf16[256,1024]{1,0:T(8,128)(2,1)} %refs_3_.1), custom_call_target="tpu_custom_call" | custom-call | tf_op jit(solution)/shard_map/pallas_call | solution.py:344
  70.6 3.9 fusion.45
  80.4 47.1 %shard_map.306.pairs = bf16[4,1024,64]{2,1,0:T(8,128)(2,1)} custom-call(bf16[1024,64]{1,0:T(8,128)(2,1)} %get-tuple-element.115.refs_0_), custom_call_target="tpu_custom_call" | custom-call | tf_op jit(solution)/shard_map/pallas_call | solution.py:344
  127.6 7.6 %fusion.11 = (f32[1024,512]{1,0:T(8,128)S(1)}, f32[1024,512]{1,0:T(8,128)}) fusion(f32[1024,512]{1,0:T(8,128)} %copy-done.21, f32[3,512]{1,0:T(4,128)S(1)} %slice.232, pred[1024]{0:T(1024)(128)(4,1)S(1)} %get-tuple-element.152, f32[512]{0:T(512)S(1)} %bitcast.164, pred[1024]{0:T(1024)(128)(4,1)S(1)} %get-tuple-element.119, f32[512]{0:T(512)S(1)} %bitcast.166, ...), kind=kLoop, calls=%fused_computation.39 | loop fusion | flops 9437184 | bytes 6310912 | tf_op jit(solution)/shard_map/jvp(jit(silu))/mul | solution.py:377
  135.3 6.4 %shard_map.307 = f32[128,512]{1,0:T(8,128)S(1)} custom-call(f32[1024,512]{1,0:T(8,128)S(1)} %get-tuple-element.117.values, bf16[4,1024,64]{2,1,0:T(8,128)(2,1)S(1)} %copy-done, f32[1024,8]{1,0:T(8,128)S(1)} %copy-done.8, f32[1,8]{1,0:T(1,128)S(1)} %get-tuple-element.173.rate, s32[1024,1]{1,0:T(8,128)S(1)} %copy-done.5, s32[1024,1]{1,0:T(8,128)S(1)} %copy-done.2), custom_call_target="tpu_custom_call" | custom-call | flops 1000000000 | bytes 5324864 | tf_op jit(solution)/shard_map/pallas_call | solution.py:264
  141.7 4.3 %collective-permute-start.1 = (f32[128,512]{1,0:T(8,128)S(1)}, f32[128,512]{1,0:T(8,128)}, u32[]{:S(2)}, u32[]{:S(2)}) collective-permute-start(f32[128,512]{1,0:T(8,128)S(1)} %shard_map.307), channel_id=1, source_target_pairs={{0,4},{4,8},{8,12},{12,16},{16,20},{20,24},{24,28},{1,5},{5,9},{9,... | collective-permute-start | bytes 786440 | tf_op jit(solution)/shard_map/ppermute | solution.py:20
  153.3 11.3 %shard_map.308 = (f32[1024,512]{1,0:T(8,128)S(1)}, f32[8,128,512]{2,1,0:T(8,128)S(1)}, f32[1024,512]{1,0:T(8,128)S(1)}) custom-call(f32[1024,512]{1,0:T(8,128)S(1)} %get-tuple-element.117.values, bf16[4,1024,64]{2,1,0:T(8,128)(2,1)S(1)} %copy-done, f32[1024,8]{1,0:T(8,128)S(1)} %copy-done.9, f32[8,1024]{1,0:T(8,128)S(1)} %fusion.73.steps_row, ...), custom_call_target="tpu_custom_call" | custom-call | flops 10000000000 | bytes 5927048 | tf_op jit(solution)/shard_map/pallas_call | solution.py:264
  168.6 6.8 %multiply_reduce_fusion.7 = (f32[1024]{0:T(1024)S(1)}, f32[1024]{0:T(1024)S(1)}, f32[1024,512]{1,0:T(8,128)}, f32[1024,512]{1,0:T(8,128)}) fusion(f32[512]{0:T(512)S(1)} %copy-done.50, f32[1024,512]{1,0:T(8,128)} %copy-done.13, f32[1024,512]{1,0:T(8,128)} %fusion.45, bf16[1024,1024]{1,0:T(8,128)(2,1)} %all-gather.3.cloned.1.call-done, ...), kind=kOutput, calls=%fused_computation.35 | convolution fusion | flops 1078982656 | bytes 11544576 | tf_op jit(solution)/shard_map/dot_general | solution.py:527
  176.0 5.0 %shard_map.309 = f32[4,2,1024]{2,1,0:T(2,128)} custom-call(f32[2,1024]{1,0:T(2,128)} %pad_maximum_fusion.7.refs_0_), custom_call_target="tpu_custom_call" | custom-call | tf_op jit(solution)/shard_map/pallas_call | solution.py:344
  181.8 4.3 %multiply_convert_fusion.1 = (bf16[1024,512]{1,0:T(8,128)(2,1)S(1)}, f32[1024,512]{1,0:T(8,128)S(1)}, f32[512]{0:T(512)S(1)}) fusion(f32[1024,512]{1,0:T(8,128)} %fusion.45, f32[1024,512]{1,0:T(8,128)} %copy-done.13, f32[1024,512]{1,0:T(8,128)} %get-tuple-element.114, f32[1024]{0:T(1024)S(1)} %fusion.36, f32[1024,512]{1,0:T(8,128)} %get-tuple-element.174, ...), kind=kLoop, calls=%fused_computation.31 | loop fusion | flops 9960960 | bytes 11546624 | tf_op jit(solution)/shard_map/convert_element_type | solution.py:589
  186.2 3.2 fusion.57
  204.2 3.4 collective-permute-start.5
  209.6 3.1 collective-permute-start.3
  213.5 19.1 %shard_map.310 = (f32[1024,512]{1,0:T(8,128)S(1)}, f32[4,1024,64]{2,1,0:T(8,128)S(1)}, f32[1024,8]{1,0:T(8,128)S(1)}, f32[1,8]{1,0:T(1,128)S(1)}, f32[1,512]{1,0:T(1,128)S(1)}) custom-call(f32[1024,512]{1,0:T(8,128)S(1)} %get-tuple-element.117.values, f32[1024,512]{1,0:T(8,128)S(1)} %get-tuple-element.124.grads, bf16[4,1024,64]{2,1,0:T(8,128)(2,1)S(1)} %copy-done, ...), custom_call_target="tpu_custom_call" | custom-call | flops 20000000000 | bytes 14315648 | tf_op jit(solution)/shard_map/pallas_call | solution.py:264
  232.7 2.6 multiply_reduce_fusion.4
  244.4 3.2 collective-permute-start.6
  252.7 4.2 %convolution_convert_fusion.2 = bf16[1024,512]{1,0:T(8,128)(2,1)} fusion(bf16[1024,512]{1,0:T(8,128)(2,1)S(1)} %scatter-add.6, f32[1024]{0:T(1024)S(1)} %copy-done.45, f32[1024]{0:T(1024)S(1)} %add_rsqrt_fusion, bf16[1024,1024]{1,0:T(8,128)(2,1)} %bitcast.131), kind=kOutput, calls=%fused_computation.43 | convolution fusion | flops 1078460416 | bytes 4202496 | tf_op jit(solution)/shard_map/dot_general | solution.py:387
  258.7 40.9 %collective-permute-done.8 = f32[1024,64]{1,0:T(8,128)} collective-permute-done((f32[1024,64]{1,0:T(8,128)}, f32[1024,64]{1,0:T(8,128)}, u32[]{:S(2)}, u32[]{:S(2)}) %collective-permute-start.8) | collective-permute-done | bytes 262176 | tf_op jit(solution)/shard_map/ppermute | solution.py:282
  299.6 3.1 multiply_reduce_fusion.12
  303.6 3.1 collective-permute-start.10
  307.0 2.8 fusion.14
  316.2 4.3 %multiply_reduce_fusion = (f32[1024]{0:T(1024)S(1)}, bf16[1024,1024]{1,0:T(8,128)(2,1)}, f32[1024,1024]{1,0:T(8,128)}) fusion(f32[1024]{0:T(1024)S(1)} %add_rsqrt_fusion, bf16[1024,1024]{1,0:T(8,128)(2,1)S(1)} %bitcast.137, f32[1024,1024]{1,0:T(8,128)S(1)} %fusion.34, f32[1024,1024]{1,0:T(8,128)S(1)} %copy-done.29, bf16[1024,512]{1,0:T(8,128)(2,1)S(1)} %scatter-add.6, ...), kind=kOutput, calls=%fused_computation.4 | convolution fusion | flops 1081080832 | bytes 18882560 | tf_op jit(solution)/shard_map/dot_general | solution.py:381
  322.0 50.2 %shard_map.311 = (bf16[4,256,1024]{2,1,0:T(8,128)(2,1)}, bf16[8,128,512]{2,1,0:T(8,128)(2,1)}, bf16[8,128,512]{2,1,0:T(8,128)(2,1)}, bf16[8,128,72]{2,1,0:T(8,128)(2,1)}, f32[8,40,128]{2,1,0:T(8,128)}) custom-call(bf16[4,256,1024]{2,1,0:T(8,128)(2,1)} %bitcast.129, bf16[8,128,512]{2,1,0:T(8,128)(2,1)} %bitcast.142, bf16[8,128,512]{2,1,0:T(8,128)(2,1)} %bitcast.143, ...), custom_call_target="tpu_custom_call" | custom-call | tf_op jit(solution)/shard_map/pallas_call | solution.py:344
  383.4 5.7 %shard_map.312 = f32[4,1,256]{2,1,0:T(1,128)} custom-call(f32[4,1,256]{2,1,0:T(1,128)} %bitcast.169), custom_call_target="tpu_custom_call" | custom-call | tf_op jit(solution)/shard_map/pallas_call | solution.py:344
  (253 shorter events, 92.5 us)
Async XLA Ops:
  7.2 55.5 %copy-start.45 = (f32[1024]{0:T(1024)S(1)}, f32[1024]{0:T(1024)}, u32[]{:S(2)}) copy-start(f32[1024]{0:T(1024)} %param.25) | copy-start | bytes 12292
  7.2 161.4 %all-gather.5.cloned.1.call-start = ((), (), s32[]{:S(2)}) async-start(), calls=%async_computation.1 | async-start | bytes 1179648 | tf_op jit(solution)/shard_map/all_gather | solution.py:441
  60.4 108.2 %all-gather.3.cloned.1.call-start = ((), (), s32[]{:S(2)}) async-start(), calls=%async_computation | async-start | bytes 2621440 | tf_op jit(solution)/shard_map/all_gather | solution.py:440
  67.5 10.8 %collective-permute-start = (f32[3,576]{1,0:T(4,128)S(1)}, f32[3,576]{1,0:T(4,128)S(1)}, u32[]{:S(2)}, u32[]{:S(2)}) collective-permute-start(f32[3,576]{1,0:T(4,128)S(1)} %pad_maximum_fusion.6), channel_id=1, source_target_pairs={{0,4},{4,8},{8,12},{12,16},{16,20},{20,24},{24,28},{1,5},{5,9},{9,... | collective-permute-start | bytes 20744 | tf_op jit(solution)/shard_map/ppermute | solution.py:20
  74.7 52.8 %copy-start.27 = (f32[1024,64]{1,0:T(8,128)}, f32[1024,64]{1,0:T(8,128)S(1)}, u32[]{:S(2)}) copy-start(f32[1024,64]{1,0:T(8,128)S(1)} %copy.102) | copy-start | bytes 786436
  74.8 52.8 %copy-start.49 = (f32[512]{0:T(512)S(1)}, f32[512]{0:T(512)}, u32[]{:S(2)}) copy-start(f32[512]{0:T(512)} %param.36) | copy-start | bytes 6148
  141.7 8.5 %collective-permute-start.1 = (f32[128,512]{1,0:T(8,128)S(1)}, f32[128,512]{1,0:T(8,128)}, u32[]{:S(2)}, u32[]{:S(2)}) collective-permute-start(f32[128,512]{1,0:T(8,128)S(1)} %shard_map.307), channel_id=1, source_target_pairs={{0,4},{4,8},{8,12},{12,16},{16,20},{20,24},{24,28},{1,5},{5,9},{9,... | collective-permute-start | bytes 786440 | tf_op jit(solution)/shard_map/ppermute | solution.py:20
  193.4 7.9 %collective-permute-start.11 = (bf16[128,512]{1,0:T(8,128)(2,1)S(1)}, bf16[128,512]{1,0:T(8,128)(2,1)S(1)}, u32[]{:S(2)}, u32[]{:S(2)}) collective-permute-start(bf16[128,512]{1,0:T(8,128)(2,1)S(1)} %get-tuple-element.139), channel_id=1, source_target_pairs={{0,4},{4,8},{8,12},{12,16},{16,20},{20,24},{24,28},{28,0},{1,5},{5... | collective-permute-start | bytes 393224 | tf_op jit(solution)/shard_map/ppermute | solution.py:282
  193.4 8.5 %collective-permute-start.12 = (bf16[128,512]{1,0:T(8,128)(2,1)S(1)}, bf16[128,512]{1,0:T(8,128)(2,1)S(1)}, u32[]{:S(2)}, u32[]{:S(2)}) collective-permute-start(bf16[128,512]{1,0:T(8,128)(2,1)S(1)} %get-tuple-element.145), channel_id=1, source_target_pairs={{0,8},{4,12},{8,16},{12,20},{16,24},{20,28},{24,0},{28,4},{1,9},{5... | collective-permute-start | bytes 393224 | tf_op jit(solution)/shard_map/ppermute | solution.py:282
  195.8 8.4 %collective-permute-start.13 = (bf16[128,512]{1,0:T(8,128)(2,1)S(1)}, bf16[128,512]{1,0:T(8,128)(2,1)S(1)}, u32[]{:S(2)}, u32[]{:S(2)}) collective-permute-start(bf16[128,512]{1,0:T(8,128)(2,1)S(1)} %get-tuple-element.144), channel_id=1, source_target_pairs={{0,12},{4,16},{8,20},{12,24},{16,28},{20,0},{24,4},{28,8},{1,13},{... | collective-permute-start | bytes 393224 | tf_op jit(solution)/shard_map/ppermute | solution.py:282
  197.2 11.7 %collective-permute-start.14 = (bf16[128,512]{1,0:T(8,128)(2,1)S(1)}, bf16[128,512]{1,0:T(8,128)(2,1)S(1)}, u32[]{:S(2)}, u32[]{:S(2)}) collective-permute-start(bf16[128,512]{1,0:T(8,128)(2,1)S(1)} %get-tuple-element.143), channel_id=1, source_target_pairs={{0,16},{4,20},{8,24},{12,28},{16,0},{20,4},{24,8},{28,12},{1,17},{... | collective-permute-start | bytes 393224 | tf_op jit(solution)/shard_map/ppermute | solution.py:282
  198.7 10.9 %collective-permute-start.15 = (bf16[128,512]{1,0:T(8,128)(2,1)S(1)}, bf16[128,512]{1,0:T(8,128)(2,1)S(1)}, u32[]{:S(2)}, u32[]{:S(2)}) collective-permute-start(bf16[128,512]{1,0:T(8,128)(2,1)S(1)} %get-tuple-element.142), channel_id=1, source_target_pairs={{0,20},{4,24},{8,28},{12,0},{16,4},{20,8},{24,12},{28,16},{1,21},{... | collective-permute-start | bytes 393224 | tf_op jit(solution)/shard_map/ppermute | solution.py:282
  201.3 11.4 %collective-permute-start.16 = (bf16[128,512]{1,0:T(8,128)(2,1)S(1)}, bf16[128,512]{1,0:T(8,128)(2,1)S(1)}, u32[]{:S(2)}, u32[]{:S(2)}) collective-permute-start(bf16[128,512]{1,0:T(8,128)(2,1)S(1)} %get-tuple-element.141), channel_id=1, source_target_pairs={{0,24},{4,28},{8,0},{12,4},{16,8},{20,12},{24,16},{28,20},{1,25},{... | collective-permute-start | bytes 393224 | tf_op jit(solution)/shard_map/ppermute | solution.py:282
  201.9 10.7 %collective-permute-start.17 = (bf16[128,512]{1,0:T(8,128)(2,1)S(1)}, bf16[128,512]{1,0:T(8,128)(2,1)S(1)}, u32[]{:S(2)}, u32[]{:S(2)}) collective-permute-start(bf16[128,512]{1,0:T(8,128)(2,1)S(1)} %get-tuple-element.140), channel_id=1, source_target_pairs={{0,28},{4,0},{8,4},{12,8},{16,12},{20,16},{24,20},{28,24},{1,29},{... | collective-permute-start | bytes 393224 | tf_op jit(solution)/shard_map/ppermute | solution.py:282
  204.2 9.3 %collective-permute-start.5 = (f32[128,512]{1,0:T(8,128)S(1)}, f32[128,512]{1,0:T(8,128)S(1)}, u32[]{:S(2)}, u32[]{:S(2)}) collective-permute-start(f32[128,512]{1,0:T(8,128)S(1)} %fusion.8), channel_id=1, source_target_pairs={{4,0},{8,4},{12,8},{16,12},{20,16},{24,20},{28,24},{5,1},{9,5},{13... | collective-permute-start | bytes 786440 | tf_op jit(solution)/shard_map/ppermute | solution.py:20
  208.9 98.0 %collective-permute-start.2 = (bf16[256,1024]{1,0:T(8,128)(2,1)}, bf16[256,1024]{1,0:T(8,128)(2,1)}, u32[]{:S(2)}, u32[]{:S(2)}) collective-permute-start(bf16[256,1024]{1,0:T(8,128)(2,1)} %get-tuple-element.136), channel_id=1, source_target_pairs={{0,1},{1,2},{2,3},{3,0},{4,5},{5,6},{6,7},{7,4},{8,9},{9,10},{10,1... | collective-permute-start | bytes 1572872 | tf_op jit(solution)/shard_map/ppermute | solution.py:282
  209.6 97.4 %collective-permute-start.3 = (bf16[256,1024]{1,0:T(8,128)(2,1)}, bf16[256,1024]{1,0:T(8,128)(2,1)}, u32[]{:S(2)}, u32[]{:S(2)}) collective-permute-start(bf16[256,1024]{1,0:T(8,128)(2,1)} %get-tuple-element.138), channel_id=1, source_target_pairs={{0,2},{1,3},{2,0},{3,1},{4,6},{5,7},{6,4},{7,5},{8,10},{9,11},{10,... | collective-permute-start | bytes 1572872 | tf_op jit(solution)/shard_map/ppermute | solution.py:282
  242.2 15.0 %collective-permute-start.7 = (f32[1024,64]{1,0:T(8,128)}, f32[1024,64]{1,0:T(8,128)}, u32[]{:S(2)}, u32[]{:S(2)}) collective-permute-start(f32[1024,64]{1,0:T(8,128)} %get-tuple-element.133), channel_id=1, source_target_pairs={{0,1},{1,2},{2,3},{3,0},{4,5},{5,6},{6,7},{7,4},{8,9},{9,10},{10,1... | collective-permute-start | bytes 786440 | tf_op jit(solution)/shard_map/ppermute | solution.py:282
  242.2 57.4 %collective-permute-start.8 = (f32[1024,64]{1,0:T(8,128)}, f32[1024,64]{1,0:T(8,128)}, u32[]{:S(2)}, u32[]{:S(2)}) collective-permute-start(f32[1024,64]{1,0:T(8,128)} %get-tuple-element.135), channel_id=1, source_target_pairs={{0,2},{1,3},{2,0},{3,1},{4,6},{5,7},{6,4},{7,5},{8,10},{9,11},{10,... | collective-permute-start | bytes 786440 | tf_op jit(solution)/shard_map/ppermute | solution.py:282
  244.4 7.3 %collective-permute-start.6 = (f32[3,512]{1,0:T(4,128)S(1)}, f32[3,512]{1,0:T(4,128)S(1)}, u32[]{:S(2)}, u32[]{:S(2)}) collective-permute-start(f32[3,512]{1,0:T(4,128)S(1)} %pad_add_fusion.2), channel_id=1, source_target_pairs={{4,0},{8,4},{12,8},{16,12},{20,16},{24,20},{28,24},{5,1},{9,5},{13... | collective-permute-start | bytes 18440 | tf_op jit(solution)/shard_map/ppermute | solution.py:20
  251.7 47.8 %collective-permute-start.9 = (f32[1024,64]{1,0:T(8,128)}, f32[1024,64]{1,0:T(8,128)}, u32[]{:S(2)}, u32[]{:S(2)}) collective-permute-start(f32[1024,64]{1,0:T(8,128)} %get-tuple-element.134), channel_id=1, source_target_pairs={{0,3},{1,0},{2,1},{3,2},{4,7},{5,4},{6,5},{7,6},{8,11},{9,8},{10,9... | collective-permute-start | bytes 786440 | tf_op jit(solution)/shard_map/ppermute | solution.py:282
  252.7 46.9 %copy-start.28 = (f32[1024,64]{1,0:T(8,128)S(1)}, f32[1024,64]{1,0:T(8,128)}, u32[]{:S(2)}) copy-start(f32[1024,64]{1,0:T(8,128)} %copy-done.27) | copy-start | bytes 786436
  257.2 49.7 %collective-permute-start.4 = (bf16[256,1024]{1,0:T(8,128)(2,1)S(1)}, bf16[256,1024]{1,0:T(8,128)(2,1)S(1)}, u32[]{:S(2)}, u32[]{:S(2)}) collective-permute-start(bf16[256,1024]{1,0:T(8,128)(2,1)S(1)} %copy-done.43), channel_id=1, source_target_pairs={{0,3},{1,0},{2,1},{3,2},{4,7},{5,4},{6,5},{7,6},{8,11},{9,8},{10,9... | collective-permute-start | bytes 1572872 | tf_op jit(solution)/shard_map/ppermute | solution.py:282
  303.6 7.0 %collective-permute-start.10 = (f32[3,64]{1,0:T(4,128)S(1)}, f32[3,64]{1,0:T(4,128)S(1)}, u32[]{:S(2)}, u32[]{:S(2)}) collective-permute-start(f32[3,64]{1,0:T(4,128)S(1)} %pad_add_fusion.3), channel_id=1, source_target_pairs={{4,0},{8,4},{12,8},{16,12},{20,16},{24,20},{28,24},{5,1},{9,5},{13... | collective-permute-start | bytes 2312 | tf_op jit(solution)/shard_map/ppermute | solution.py:20
  (54 other events, 317.5 us)
Sparse Core Ops, SparseCore 0:
  60.5 23.7 all-gather.4
  85.9 54.1 all-gather.2

commit v3 on v2

--- a/solution.py
+++ b/solution.py
@@ -305,20 +305,37 @@
             )
     pl.semaphore_wait(barrier, sum(lax.axis_size(axis) - 1 for axis in axes))
     copies = []
+    relays = []
     slot = 0
+
+    def push(item, source, place, axis, peer, slot):
+        return pltpu.make_async_remote_copy(
+            src_ref=source,
+            dst_ref=targets[item].at[place],
+            send_sem=send.at[slot],
+            recv_sem=receive.at[slot],
+            device_id={axis: peer},
+            device_id_type=pl.DeviceIdType.MESH,
+        )
+
     for item, (axis, blocks) in enumerate(plan):
         size = lax.axis_size(axis)
         me = lax.axis_index(axis)
-        for hop in range(1, size):
+        paired = not blocks and axis == "dp" and size % 2 == 0
+        for hop in (range(1, size) if not paired else range(2, size, 2)):
             peer = lax.rem(me + hop, size)
-            copy = pltpu.make_async_remote_copy(
-                src_ref=sources[item].at[peer] if blocks else sources[item],
-                dst_ref=targets[item].at[me],
-                send_sem=send.at[slot],
-                recv_sem=receive.at[slot],
-                device_id={axis: peer},
-                device_id_type=pl.DeviceIdType.MESH,
+            copy = push(
+                item, sources[item].at[peer] if blocks else sources[item], me, axis, peer, slot
             )
+            copy.start()
+            if paired:
+                relays.append((copy, item, axis, lax.rem(me - hop + size, size), slot + 1))
+                slot += 1
+            copies.append(copy)
+            slot += 1
+        if paired:
+            partner = me + 1 - 2 * lax.rem(me, 2)
+            copy = push(item, sources[item], me, axis, partner, slot)
             copy.start()
             copies.append(copy)
             slot += 1
@@ -327,8 +344,19 @@
         )
         own.start()
         copies.append(own)
+    for copy, item, axis, origin, place in relays:
+        copy.wait_recv()
+        me = lax.axis_index(axis)
+        partner = me + 1 - 2 * lax.rem(me, 2)
+        onward = push(item, targets[item].at[origin], origin, axis, partner, place)
+        onward.start()
+        copies.append(onward)
+    relayed = [copy for copy, *_ in relays]
     for copy in copies:
-        copy.wait()
+        if any(copy is other for other in relayed):
+            copy.wait_send()
+        else:
+            copy.wait()
 
 
 def transfer(items, number):
@@ -434,11 +462,6 @@
         item.reshape((-1, item.shape[2]))
         for item in (gate_full, value_full, rest_full, hidden_rows)
     )
-    grad_source, out_source, hidden_rows = lax.optimization_barrier(
-        (out_grad, out_weight, hidden_rows)
-    )
-    grad_rows = lax.all_gather(grad_source, "tensor", axis=0, tiled=True)
-    out_full = lax.all_gather(out_source, "dp", axis=0, tiled=True)
     hidden_float = hidden_rows.astype(jnp.float32)
     scale = lax.rsqrt(jnp.mean(hidden_float * hidden_float, axis=1, keepdims=True) + epsilon)
     normed = hidden_float * scale
@@ -473,6 +496,11 @@
     pair, pair_back = jax.vjp(convolve, pair_in, pair_rim, pair_kernel, pair_offset)
     values, value_back = jax.vjp(convolve, value_in, value_rim, conv_value, conv_value_bias)
     (pairs,) = transfer([(pair.astype(jnp.bfloat16), "tensor", False)], 2)
+    grad_source, out_source, pairs = lax.optimization_barrier(
+        (out_grad, out_weight, pairs)
+    )
+    grad_rows = lax.all_gather(grad_source, "tensor", axis=0, tiled=True)
+    out_full = lax.all_gather(out_source, "dp", axis=0, tiled=True)
     steps = jax.nn.softplus(step_in + step_bias[None, :])
     rate = -jnp.exp(decay_log)
     turns = group_rows // SPAN

time: 406 us -> 411 us (1.012)
  waiting for transfers between devices: 41.9 us -> 75.5 us
  Pallas kernels: 195 us -> 173 us
  starting transfers between devices: 31.8 us -> 26.8 us
  other arithmetic: 46.9 us -> 42.6 us
    all_gather x1, waiting for transfers between devices: 0.01 us -> 24.9 us  [body(): grad_rows = lax.all_gather(grad_source, 'tensor', axis=0, tiled=True)]
    pallas_call x5, Pallas kernels: 158 us -> 136 us  [transfer(): pl.pallas_call(partial(transfer_kernel, plan), in_specs=[pl.BlockSpec(mem...]
    ppermute x5, starting transfers between devices: 16 us -> 11.2 us  [from_behind(): lax.ppermute(value, axis, [(source, source + steps) for source in range(l...]
    ppermute x13, waiting for transfers between devices: 41.3 us -> 45.8 us  [exchange_sum(): lax.ppermute(sent, axis, [(i, (i + hop) % count) for i in range(count)])]
    mul x1, other arithmetic: 7.61 us -> 3.46 us  [conv_apply(): return jax.nn.silu(total)]
    ppermute x5, waiting for transfers between devices: 0.59 us -> 4.72 us  [from_behind(): lax.ppermute(value, axis, [(source, source + steps) for source in range(l...]
  transfers between devices with their start and end apart: 20 -> 20, of which waited for: 3 -> 8; matrix products, arithmetic and copies ran while one was open for 14% -> 10% of each run, Pallas kernels for 21% -> 9%
where the time goes in v3:
time: 411 us; the launch traced here: 407 us
  Pallas kernels  173 us (42%)
  waiting for transfers between devices  75.5 us (18%)
  other arithmetic  42.6 us (10%)
  local copies, waits for them, and re-layouts  38.7 us (9%)
  matrix products  35.7 us (9%)
  starting transfers between devices  26.8 us (7%)
  between operations  15 us (4%)
    pallas_call x5, Pallas kernels, transfer(): pl.pallas_call(partial(transfer_kernel, plan), in_specs=[pl.BlockSpec(mem...  136 us
    ppermute x13, waiting for transfers between devices, exchange_sum(): lax.ppermute(sent, axis, [(i, (i + hop) % count) for i in range(count)])  45.8 us
    pallas_call x3, Pallas kernels, scan_call(): pl.pallas_call(kernel, grid=(turns,), in_specs=[spec(a.shape, kind) for a...  37.2 us
    all_gather x1, waiting for transfers between devices, body(): grad_rows = lax.all_gather(grad_source, 'tensor', axis=0, tiled=True)  24.9 us
    unnamed x123, local copies, waits for them, and re-layouts  17.6 us
    ppermute x13, starting transfers between devices, exchange_sum(): lax.ppermute(sent, axis, [(i, (i + hop) % count) for i in range(count)])  15.5 us
    dot_general x4, matrix products, contract_last(): lax.dot_general(left, right, (((1,), (1,)), ((), ())), preferred_element_...  11.8 us
    ppermute x5, starting transfers between devices, from_behind(): lax.ppermute(value, axis, [(source, source + steps) for source in range(l...  11.2 us
  transfers between devices with their start and end apart: 20, of which 8 were waited for; matrix products, arithmetic and copies ran while one was open for 10% of the time, Pallas kernels for 9%

profile of v3, /device:TPU:10, one launch (start us, length us, event | category | flops | bytes accessed | tf_op | source)
XLA Modules:
  0.0 407.4 jit_solution(15959757678316610696)
XLA Ops:
  10.4 49.9 %shard_map.305 = (bf16[8,128,512]{2,1,0:T(8,128)(2,1)}, bf16[8,128,512]{2,1,0:T(8,128)(2,1)}, bf16[8,128,72]{2,1,0:T(8,128)(2,1)}, bf16[4,256,1024]{2,1,0:T(8,128)(2,1)}) custom-call(bf16[128,512]{1,0:T(8,128)(2,1)} %refs_0_.1, bf16[128,512]{1,0:T(8,128)(2,1)} %refs_1_.1, bf16[128,72]{1,0:T(8,128)(2,1)} %pad_maximum_fusion.5.refs_2_, bf16[256,1024]{1,0:T(8,128)(2,1)} %refs_3_.1), custom_call_target="tpu_custom_call" | custom-call | tf_op jit(solution)/shard_map/pallas_call | solution.py:372
  75.5 25.2 %shard_map.306.pairs = bf16[4,1024,64]{2,1,0:T(8,128)(2,1)} custom-call(bf16[1024,64]{1,0:T(8,128)(2,1)} %get-tuple-element.117.refs_0_), custom_call_target="tpu_custom_call" | custom-call | tf_op jit(solution)/shard_map/pallas_call | solution.py:372
  105.1 4.0 fusion.57
  109.2 3.5 fusion.10
  112.7 6.4 %shard_map.307 = f32[128,512]{1,0:T(8,128)S(1)} custom-call(f32[1024,512]{1,0:T(8,128)S(1)} %get-tuple-element.115.values, bf16[4,1024,64]{2,1,0:T(8,128)(2,1)S(1)} %copy-done, f32[1024,8]{1,0:T(8,128)S(1)} %copy-done.8, f32[1,8]{1,0:T(1,128)S(1)} %get-tuple-element.179.rate, s32[1024,1]{1,0:T(8,128)S(1)} %copy-done.5, s32[1024,1]{1,0:T(8,128)S(1)} %copy-done.2), custom_call_target="tpu_custom_call" | custom-call | flops 1000000000 | bytes 5324864 | tf_op jit(solution)/shard_map/pallas_call | solution.py:264
  130.0 11.3 %shard_map.308 = (f32[1024,512]{1,0:T(8,128)S(1)}, f32[8,128,512]{2,1,0:T(8,128)S(1)}, f32[1024,512]{1,0:T(8,128)S(1)}) custom-call(f32[1024,512]{1,0:T(8,128)S(1)} %get-tuple-element.115.values, bf16[4,1024,64]{2,1,0:T(8,128)(2,1)S(1)} %copy-done, f32[1024,8]{1,0:T(8,128)S(1)} %copy-done.9, f32[8,1024]{1,0:T(8,128)S(1)} %fusion.80.steps_row, ...), custom_call_target="tpu_custom_call" | custom-call | flops 10000000000 | bytes 5927048 | tf_op jit(solution)/shard_map/pallas_call | solution.py:264
  145.3 24.9 %all-gather.3.cloned.1.call-done = bf16[1024,1024]{1,0:T(8,128)(2,1)} async-done(((bf16[256,1024]{1,0:T(8,128)(2,1)}), bf16[1024,1024]{1,0:T(8,128)(2,1)}) %all-gather.3.cloned.1.call-update) | async-done | bytes 2097168 | tf_op jit(solution)/shard_map/all_gather | solution.py:502
  170.2 6.8 %multiply_reduce_fusion.8 = (f32[1024]{0:T(1024)S(1)}, f32[1024]{0:T(1024)S(1)}, f32[1024,512]{1,0:T(8,128)}, f32[1024,512]{1,0:T(8,128)}) fusion(f32[512]{0:T(512)S(1)} %copy-done.50, f32[1024,512]{1,0:T(8,128)} %copy-done.13, f32[1024,512]{1,0:T(8,128)} %fusion.57, bf16[1024,1024]{1,0:T(8,128)(2,1)} %all-gather.3.cloned.1.call-done, ...), kind=kOutput, calls=%fused_computation.35 | convolution fusion | flops 1078982656 | bytes 11544576 | tf_op jit(solution)/shard_map/dot_general | solution.py:555
  177.6 6.6 %shard_map.309 = f32[4,2,1024]{2,1,0:T(2,128)} custom-call(f32[2,1024]{1,0:T(2,128)} %pad_maximum_fusion.7.refs_0_), custom_call_target="tpu_custom_call" | custom-call | tf_op jit(solution)/shard_map/pallas_call | solution.py:372
  185.0 3.7 convolution_convert_fusion.1
  196.2 3.2 fusion.58
  208.8 3.1 collective-permute-start.3
  212.8 19.5 %shard_map.310 = (f32[1024,512]{1,0:T(8,128)S(1)}, f32[4,1024,64]{2,1,0:T(8,128)S(1)}, f32[1024,8]{1,0:T(8,128)S(1)}, f32[1,8]{1,0:T(1,128)S(1)}, f32[1,512]{1,0:T(1,128)S(1)}) custom-call(f32[1024,512]{1,0:T(8,128)S(1)} %get-tuple-element.115.values, f32[1024,512]{1,0:T(8,128)S(1)} %get-tuple-element.124.grads, bf16[4,1024,64]{2,1,0:T(8,128)(2,1)S(1)} %copy-done, ...), custom_call_target="tpu_custom_call" | custom-call | flops 20000000000 | bytes 14315648 | tf_op jit(solution)/shard_map/pallas_call | solution.py:264
  232.3 2.7 multiply_reduce_fusion.5
  255.2 25.5 %collective-permute-done.4 = bf16[256,1024]{1,0:T(8,128)(2,1)} collective-permute-done((bf16[256,1024]{1,0:T(8,128)(2,1)}, bf16[256,1024]{1,0:T(8,128)(2,1)}, u32[]{:S(2)}, u32[]{:S(2)}) %collective-permute-start.4) | collective-permute-done | bytes 524320 | tf_op jit(solution)/shard_map/ppermute | solution.py:282
  280.7 3.1 fusion.13
  283.8 5.0 %collective-permute-done.7 = f32[1024,64]{1,0:T(8,128)} collective-permute-done((f32[1024,64]{1,0:T(8,128)}, f32[1024,64]{1,0:T(8,128)}, u32[]{:S(2)}, u32[]{:S(2)}) %collective-permute-start.7) | collective-permute-done | bytes 262176 | tf_op jit(solution)/shard_map/ppermute | solution.py:282
  288.8 10.8 %collective-permute-done.8 = f32[1024,64]{1,0:T(8,128)} collective-permute-done((f32[1024,64]{1,0:T(8,128)}, f32[1024,64]{1,0:T(8,128)}, u32[]{:S(2)}, u32[]{:S(2)}) %collective-permute-start.8) | collective-permute-done | bytes 262176 | tf_op jit(solution)/shard_map/ppermute | solution.py:282
  299.6 2.9 collective-permute-done.9
  302.5 3.0 multiply_reduce_fusion.13
  307.3 3.2 collective-permute-start.10
  315.6 5.4 %bitcast_multiply_fusion = (f32[1024,1024]{1,0:T(8,128)}, bf16[1024,1024]{1,0:T(8,128)(2,1)S(1)}, bf16[1024,1024]{1,0:T(8,128)(2,1)}, f32[1024]{0:T(1024)S(1)}) fusion(f32[1024]{0:T(1024)S(1)} %bitcast.187, bf16[4,256,1024]{2,1,0:T(8,128)(2,1)S(1)} %copy-done.23, f32[1024]{0:T(1024)S(1)} %copy-done.45, f32[1024,1024]{1,0:T(8,128)S(1)} %fusion.33, ...), kind=kOutput, calls=%fused_computation | convolution fusion | flops 1083177984 | bytes 20983808 | tf_op jit(solution)/shard_map/dot_general | solution.py:409
  327.7 48.9 %shard_map.311 = (bf16[4,256,1024]{2,1,0:T(8,128)(2,1)}, bf16[8,128,512]{2,1,0:T(8,128)(2,1)}, bf16[8,128,512]{2,1,0:T(8,128)(2,1)}, bf16[8,128,72]{2,1,0:T(8,128)(2,1)}, f32[8,40,128]{2,1,0:T(8,128)}) custom-call(bf16[4,256,1024]{2,1,0:T(8,128)(2,1)} %bitcast.153, bf16[8,128,512]{2,1,0:T(8,128)(2,1)} %bitcast.157, bf16[8,128,512]{2,1,0:T(8,128)(2,1)} %bitcast.156, ...), custom_call_target="tpu_custom_call" | custom-call | tf_op jit(solution)/shard_map/pallas_call | solution.py:372
  387.9 5.4 %shard_map.312 = f32[4,1,256]{2,1,0:T(1,128)} custom-call(f32[4,1,256]{2,1,0:T(1,128)} %bitcast.186), custom_call_target="tpu_custom_call" | custom-call | tf_op jit(solution)/shard_map/pallas_call | solution.py:372
  (253 shorter events, 108.6 us)
Async XLA Ops:
  7.2 55.4 %copy-start.45 = (f32[1024]{0:T(1024)S(1)}, f32[1024]{0:T(1024)}, u32[]{:S(2)}) copy-start(f32[1024]{0:T(1024)} %param.25) | copy-start | bytes 12292
  7.2 138.1 %all-gather.5.cloned.1.call-start = ((), (), s32[]{:S(2)}) async-start(), calls=%async_computation.1 | async-start | bytes 1179648 | tf_op jit(solution)/shard_map/all_gather | solution.py:503
  64.3 40.7 %copy-start.37 = (f32[1024,72]{0,1:T(8,128)}, f32[1024,72]{0,1:T(8,128)S(1)}, u32[]{:S(2)}) copy-start(f32[1024,72]{0,1:T(8,128)S(1)} %fusion.56) | copy-start | bytes 884740
  68.4 5.0 %collective-permute-start = (f32[3,576]{1,0:T(4,128)S(1)}, f32[3,576]{1,0:T(4,128)S(1)}, u32[]{:S(2)}, u32[]{:S(2)}) collective-permute-start(f32[3,576]{1,0:T(4,128)S(1)} %pad_maximum_fusion.6), channel_id=1, source_target_pairs={{0,4},{4,8},{8,12},{12,16},{16,20},{20,24},{24,28},{1,5},{5,9},{9,... | collective-permute-start | bytes 20744 | tf_op jit(solution)/shard_map/ppermute | solution.py:20
  100.7 69.5 %all-gather.3.cloned.1.call-start = ((), (), s32[]{:S(2)}) async-start(), calls=%async_computation | async-start | bytes 2621440 | tf_op jit(solution)/shard_map/all_gather | solution.py:502
  119.0 7.8 %collective-permute-start.1 = (f32[128,512]{1,0:T(8,128)S(1)}, f32[128,512]{1,0:T(8,128)}, u32[]{:S(2)}, u32[]{:S(2)}) collective-permute-start(f32[128,512]{1,0:T(8,128)S(1)} %shard_map.307), channel_id=1, source_target_pairs={{0,4},{4,8},{8,12},{12,16},{16,20},{20,24},{24,28},{1,5},{5,9},{9,... | collective-permute-start | bytes 786440 | tf_op jit(solution)/shard_map/ppermute | solution.py:20
  188.9 13.1 %collective-permute-start.11 = (bf16[128,512]{1,0:T(8,128)(2,1)S(1)}, bf16[128,512]{1,0:T(8,128)(2,1)S(1)}, u32[]{:S(2)}, u32[]{:S(2)}) collective-permute-start(bf16[128,512]{1,0:T(8,128)(2,1)S(1)} %get-tuple-element.142), channel_id=1, source_target_pairs={{0,4},{4,8},{8,12},{12,16},{16,20},{20,24},{24,28},{28,0},{1,5},{5... | collective-permute-start | bytes 393224 | tf_op jit(solution)/shard_map/ppermute | solution.py:282
  188.9 13.7 %collective-permute-start.12 = (bf16[128,512]{1,0:T(8,128)(2,1)S(1)}, bf16[128,512]{1,0:T(8,128)(2,1)S(1)}, u32[]{:S(2)}, u32[]{:S(2)}) collective-permute-start(bf16[128,512]{1,0:T(8,128)(2,1)S(1)} %get-tuple-element.148), channel_id=1, source_target_pairs={{0,8},{4,12},{8,16},{12,20},{16,24},{20,28},{24,0},{28,4},{1,9},{5... | collective-permute-start | bytes 393224 | tf_op jit(solution)/shard_map/ppermute | solution.py:282
  190.5 14.5 %collective-permute-start.13 = (bf16[128,512]{1,0:T(8,128)(2,1)S(1)}, bf16[128,512]{1,0:T(8,128)(2,1)S(1)}, u32[]{:S(2)}, u32[]{:S(2)}) collective-permute-start(bf16[128,512]{1,0:T(8,128)(2,1)S(1)} %get-tuple-element.147), channel_id=1, source_target_pairs={{0,12},{4,16},{8,20},{12,24},{16,28},{20,0},{24,4},{28,8},{1,13},{... | collective-permute-start | bytes 393224 | tf_op jit(solution)/shard_map/ppermute | solution.py:282
  191.7 16.4 %collective-permute-start.14 = (bf16[128,512]{1,0:T(8,128)(2,1)S(1)}, bf16[128,512]{1,0:T(8,128)(2,1)S(1)}, u32[]{:S(2)}, u32[]{:S(2)}) collective-permute-start(bf16[128,512]{1,0:T(8,128)(2,1)S(1)} %get-tuple-element.146), channel_id=1, source_target_pairs={{0,16},{4,20},{8,24},{12,28},{16,0},{20,4},{24,8},{28,12},{1,17},{... | collective-permute-start | bytes 393224 | tf_op jit(solution)/shard_map/ppermute | solution.py:282
  193.4 15.4 %collective-permute-start.15 = (bf16[128,512]{1,0:T(8,128)(2,1)S(1)}, bf16[128,512]{1,0:T(8,128)(2,1)S(1)}, u32[]{:S(2)}, u32[]{:S(2)}) collective-permute-start(bf16[128,512]{1,0:T(8,128)(2,1)S(1)} %get-tuple-element.145), channel_id=1, source_target_pairs={{0,20},{4,24},{8,28},{12,0},{16,4},{20,8},{24,12},{28,16},{1,21},{... | collective-permute-start | bytes 393224 | tf_op jit(solution)/shard_map/ppermute | solution.py:282
  202.0 9.9 %collective-permute-start.16 = (bf16[128,512]{1,0:T(8,128)(2,1)S(1)}, bf16[128,512]{1,0:T(8,128)(2,1)S(1)}, u32[]{:S(2)}, u32[]{:S(2)}) collective-permute-start(bf16[128,512]{1,0:T(8,128)(2,1)S(1)} %get-tuple-element.144), channel_id=1, source_target_pairs={{0,24},{4,28},{8,0},{12,4},{16,8},{20,12},{24,16},{28,20},{1,25},{... | collective-permute-start | bytes 393224 | tf_op jit(solution)/shard_map/ppermute | solution.py:282
  202.7 9.2 %collective-permute-start.17 = (bf16[128,512]{1,0:T(8,128)(2,1)S(1)}, bf16[128,512]{1,0:T(8,128)(2,1)S(1)}, u32[]{:S(2)}, u32[]{:S(2)}) collective-permute-start(bf16[128,512]{1,0:T(8,128)(2,1)S(1)} %get-tuple-element.143), channel_id=1, source_target_pairs={{0,28},{4,0},{8,4},{12,8},{16,12},{20,16},{24,20},{28,24},{1,29},{... | collective-permute-start | bytes 393224 | tf_op jit(solution)/shard_map/ppermute | solution.py:282
  205.0 7.8 %collective-permute-start.5 = (f32[128,512]{1,0:T(8,128)S(1)}, f32[128,512]{1,0:T(8,128)S(1)}, u32[]{:S(2)}, u32[]{:S(2)}) collective-permute-start(f32[128,512]{1,0:T(8,128)S(1)} %fusion.7), channel_id=1, source_target_pairs={{4,0},{8,4},{12,8},{16,12},{20,16},{24,20},{28,24},{5,1},{9,5},{13... | collective-permute-start | bytes 786440 | tf_op jit(solution)/shard_map/ppermute | solution.py:20
  208.1 45.5 %collective-permute-start.2 = (bf16[256,1024]{1,0:T(8,128)(2,1)}, bf16[256,1024]{1,0:T(8,128)(2,1)}, u32[]{:S(2)}, u32[]{:S(2)}) collective-permute-start(bf16[256,1024]{1,0:T(8,128)(2,1)} %get-tuple-element.139), channel_id=1, source_target_pairs={{0,1},{1,2},{2,3},{3,0},{4,5},{5,6},{6,7},{7,4},{8,9},{9,10},{10,1... | collective-permute-start | bytes 1572872 | tf_op jit(solution)/shard_map/ppermute | solution.py:282
  208.8 46.5 %collective-permute-start.3 = (bf16[256,1024]{1,0:T(8,128)(2,1)}, bf16[256,1024]{1,0:T(8,128)(2,1)}, u32[]{:S(2)}, u32[]{:S(2)}) collective-permute-start(bf16[256,1024]{1,0:T(8,128)(2,1)} %get-tuple-element.141), channel_id=1, source_target_pairs={{0,2},{1,3},{2,0},{3,1},{4,6},{5,7},{6,4},{7,5},{8,10},{9,11},{10,... | collective-permute-start | bytes 1572872 | tf_op jit(solution)/shard_map/ppermute | solution.py:282
  211.9 68.9 %collective-permute-start.4 = (bf16[256,1024]{1,0:T(8,128)(2,1)}, bf16[256,1024]{1,0:T(8,128)(2,1)}, u32[]{:S(2)}, u32[]{:S(2)}) collective-permute-start(bf16[256,1024]{1,0:T(8,128)(2,1)} %get-tuple-element.140), channel_id=1, source_target_pairs={{0,3},{1,0},{2,1},{3,2},{4,7},{5,4},{6,5},{7,6},{8,11},{9,8},{10,9... | collective-permute-start | bytes 1572872 | tf_op jit(solution)/shard_map/ppermute | solution.py:282
  241.9 46.9 %collective-permute-start.7 = (f32[1024,64]{1,0:T(8,128)}, f32[1024,64]{1,0:T(8,128)}, u32[]{:S(2)}, u32[]{:S(2)}) collective-permute-start(f32[1024,64]{1,0:T(8,128)} %get-tuple-element.136), channel_id=1, source_target_pairs={{0,1},{1,2},{2,3},{3,0},{4,5},{5,6},{6,7},{7,4},{8,9},{9,10},{10,1... | collective-permute-start | bytes 786440 | tf_op jit(solution)/shard_map/ppermute | solution.py:282
  243.9 6.6 %collective-permute-start.6 = (f32[3,512]{1,0:T(4,128)S(1)}, f32[3,512]{1,0:T(4,128)S(1)}, u32[]{:S(2)}, u32[]{:S(2)}) collective-permute-start(f32[3,512]{1,0:T(4,128)S(1)} %pad_add_fusion.2), channel_id=1, source_target_pairs={{4,0},{8,4},{12,8},{16,12},{20,16},{24,20},{28,24},{5,1},{9,5},{13... | collective-permute-start | bytes 18440 | tf_op jit(solution)/shard_map/ppermute | solution.py:20
  250.5 49.2 %collective-permute-start.8 = (f32[1024,64]{1,0:T(8,128)}, f32[1024,64]{1,0:T(8,128)}, u32[]{:S(2)}, u32[]{:S(2)}) collective-permute-start(f32[1024,64]{1,0:T(8,128)} %get-tuple-element.138), channel_id=1, source_target_pairs={{0,2},{1,3},{2,0},{3,1},{4,6},{5,7},{6,4},{7,5},{8,10},{9,11},{10,... | collective-permute-start | bytes 786440 | tf_op jit(solution)/shard_map/ppermute | solution.py:282
  253.4 49.1 %copy-start.29 = (f32[1024,64]{1,0:T(8,128)S(1)}, f32[1024,64]{1,0:T(8,128)}, u32[]{:S(2)}) copy-start(f32[1024,64]{1,0:T(8,128)} %copy-done.28) | copy-start | bytes 786436
  253.4 49.1 %copy-start.31 = (f32[1024,64]{1,0:T(8,128)S(1)}, f32[1024,64]{1,0:T(8,128)}, u32[]{:S(2)}) copy-start(f32[1024,64]{1,0:T(8,128)} %get-tuple-element.118) | copy-start | bytes 786436
  253.6 48.9 %collective-permute-start.9 = (f32[1024,64]{1,0:T(8,128)}, f32[1024,64]{1,0:T(8,128)S(1)}, u32[]{:S(2)}, u32[]{:S(2)}) collective-permute-start(f32[1024,64]{1,0:T(8,128)} %get-tuple-element.137), channel_id=1, source_target_pairs={{0,3},{1,0},{2,1},{3,2},{4,7},{5,4},{6,5},{7,6},{8,11},{9,8},{10,9... | collective-permute-start | bytes 786440 | tf_op jit(solution)/shard_map/ppermute | solution.py:282
  307.3 5.0 %collective-permute-start.10 = (f32[3,64]{1,0:T(4,128)S(1)}, f32[3,64]{1,0:T(4,128)S(1)}, u32[]{:S(2)}, u32[]{:S(2)}) collective-permute-start(f32[3,64]{1,0:T(4,128)S(1)} %pad_add_fusion.3), channel_id=1, source_target_pairs={{4,0},{8,4},{12,8},{16,12},{20,16},{24,20},{28,24},{5,1},{9,5},{13... | collective-permute-start | bytes 2312 | tf_op jit(solution)/shard_map/ppermute | solution.py:20
  (52 other events, 420.3 us)
Sparse Core Ops, SparseCore 0:
  100.8 23.3 all-gather.4
  125.8 44.3 all-gather.2
